TPU v7x, 32 devices: a whole 2x2x4 slice. The times are simulated.
32 devices in a mesh: group: 4 (over y, x), member: 8 (over z, core).
Axes of the slice: x: 2, y: 2, z: 4, core: 2. Of those that a mesh axis runs over, the one named last changes fastest.
Arguments:
- queries: float32 [256, 768], P(('group', 'member')), may hold values from -6 to 6
- centroids: float32 [1024, 768], P(('group', 'member')), may hold values from -0.21875 to 0.21875
- stored: float32 [16, 2048, 768], P('group', 'member'), may hold values from -0.21875 to 0.21875
- vector_ids: int32 [16, 2048], P('group', 'member'), may hold values from -1 to 32767, as said below
- list_home: int32 [16], replicated, may hold values from 0 to 15, as said below
- probes: int32 [4, 3, 4], replicated, may hold values from 0 to 15, as said below
Outputs:
- coarse_best: float32 [256], P(('group', 'member'))
- fine_best: float32 [3, 256], P(None, ('group', 'member'))
Inputs may be any that keep to these rules, and one draw needn't show every extreme that they name: A permutation: list l is stored at slot list_home[l], and slot t belongs to group t // 4. `probes`: for each block and step the 4 probed lists are stored in 4 different groups, one in each. `vector_ids`: ids are distinct where not -1; each list has its valid vectors first, 256 or more of them.
All inputs are finite; a program needn't handle non-finite values.
Results may differ from a plain program's by a relative error of at most 0.0003.
Values sent between devices are 32-bit elements; how exact they have to be, the bound alone decides.
No kernel may reach another device: no remote copies, remote signals or barrier semaphores. Data moves between devices by JAX's collectives and lax.ppermute only.
A program may use at most 64 MiB of HBM per device.

v0:
```python
import jax
import jax.numpy as jnp
from jax import lax
from jax.sharding import PartitionSpec as P

D = 768
STEPS = 3


def shifted(value, axis, steps):
    count = lax.axis_size(axis)
    pairs = [(source, (source + steps) % count) for source in range(count)]
    return lax.ppermute(value, axis, pairs)


def local(queries, centroids, stored, vector_ids, list_home, probes):
    groups = lax.axis_size("group")
    member_pos = lax.axis_index("member")
    group_pos = lax.axis_index("group")
    rows_dev = queries.shape[0]
    lowest = jnp.float32(-1e30)
    highest = lax.Precision.HIGHEST
    group_block = lax.all_gather(queries, "member", axis=0, tiled=True)
    group_centroids = lax.all_gather(centroids, "member", axis=0, tiled=True)

    def travel(visit_index, carry):
        query_block, best_seen = carry
        scores = jnp.einsum(
            "qd,cd->qc",
            query_block,
            group_centroids,
            preferred_element_type=jnp.float32,
            precision=highest,
        )
        best_seen = jnp.maximum(best_seen, jnp.max(scores, axis=1))
        return shifted((query_block, best_seen), "group", 1)

    start_best = jnp.full((rows_dev,), lowest, jnp.float32)
    moved_back, coarse_best = lax.fori_loop(0, groups, travel, (queries, start_best))
    lists_here = stored.shape[0]
    slot_ids = list_home[probes]
    at_home = slot_ids // lists_here == group_pos
    local_slot = jnp.sum(jnp.where(at_home, slot_ids - group_pos * lists_here, 0), axis=2)
    results = []
    outgoing = jnp.take(stored, local_slot, axis=0)
    marks_out = jnp.take(vector_ids, local_slot, axis=0)
    pieces, marks_in = (
        lax.all_to_all(outgoing, "group", split_axis=0, concat_axis=0, tiled=True),
        lax.all_to_all(marks_out, "group", split_axis=0, concat_axis=0, tiled=True),
    )
    for probe_step in range(STEPS):
        score_pieces = pieces[:, probe_step]
        score_marks_in = marks_in[:, probe_step]
        vectors = score_pieces.reshape(-1, D)
        score_scores = jnp.einsum(
            "qd,rd->qr", group_block, vectors, preferred_element_type=jnp.float32, precision=highest
        )
        score_scores = jnp.where(score_marks_in.reshape(-1)[None, :] >= 0, score_scores, lowest)
        results.append(jnp.max(score_scores, axis=1))
    fine_partial = jnp.stack(results)
    fine_all = lax.pmax(fine_partial, "member")
    fine_best = lax.dynamic_slice_in_dim(fine_all, member_pos * rows_dev, rows_dev, 1)
    return (coarse_best, fine_best)


def solution(mesh):
    placed = (
        P(("group", "member"), None),
        P(("group", "member"), None),
        P("group", "member", None),
        P("group", "member"),
        P(),
        P(),
    )
    return jax.shard_map(
        local,
        mesh=mesh,
        in_specs=placed,
        out_specs=(P(("group", "member")), P(None, ("group", "member"))),
        check_vma=False,
    )
```

profile of v0, /device:TPU:0, one launch (start us, length us, event | category | flops | bytes accessed | tf_op | source)
XLA Modules:
  0.0 201.8 jit_solution(5528428097105693312)
XLA Ops:
  0.7 0.8 compare_select_fusion
  1.6 0.8 gather_fusion
  2.8 0.6 gather_fusion.1
  3.4 0.7 broadcast_select_fusion.1
  4.1 5.2 %all-to-all-start = ((s32[4,3,256]{2,1,0:T(4,128)}), s32[4,3,256]{2,1,0:T(4,128)S(1)}, u32[]{:S(2)}, u32[]{:S(2)}) async-start(s32[4,3,256]{2,1,0:T(4,128)} %broadcast_select_fusion.1), calls=%async_computation | async-start | bytes 32768 | tf_op jit(solution)/shard_map/all_to_all | solution.py:49
  9.2 4.8 %gather_fusion.2 = f32[12,256,768]{2,1,0:T(8,128)} fusion(f32[4,256,768]{2,1,0:T(8,128)S(1)} %copy-done, s32[1024]{0:T(1024)S(1)} %pad_clamp_fusion), kind=kCustom, calls=%fused_computation.2 | custom fusion | bytes 18874416 | tf_op jit(solution)/shard_map/jit(_take)/gather | solution.py:45
  14.0 8.3 %broadcast_select_fusion = f32[4,3,256,768]{3,2,1,0:T(8,128)} fusion(f32[4,3,256,768]{3,2,1,0:T(8,128)} %bitcast.23, pred[4,3]{1,0:T(4,128)(4,1)S(1)} %compare_and_fusion), kind=kLoop, calls=%fused_computation.4 | loop fusion | flops 2359296 | bytes 18874380 | tf_op jit(solution)/shard_map/jit(_take)/select_n | solution.py:45
  22.3 5.9 %all-to-all-start.1 = ((f32[4,3,256,768]{3,2,1,0:T(8,128)}), f32[4,3,256,768]{3,2,1,0:T(8,128)}, u32[]{:S(2)}, u32[]{:S(2)}) async-start(f32[4,3,256,768]{3,2,1,0:T(8,128)} %broadcast_select_fusion), calls=%async_computation.1 | async-start | bytes 18874368 | tf_op jit(solution)/shard_map/all_to_all | solution.py:48
  28.3 16.8 %all_gather.6 = f32[256,768]{1,0:T(8,128)} all-gather(f32[32,768]{1,0:T(8,128)S(1)} %copy-done.5), channel_id=1, replica_groups=mesh['group'=4,'member'=8] {'member'}, dimensions={0}, use_global_device_ids=true | all-gather | bytes 884736 | tf_op jit(solution)/shard_map/all_gather | solution.py:24
  45.1 109.2 %while.12 = (s32[]{:T(128)}, f32[8,768]{1,0:T(8,128)S(1)}, f32[8]{0:T(128)S(1)}, f32[256,768]{1,0:T(8,128)}, s32[]{:T(128)}) while((s32[]{:T(128)}, f32[8,768]{1,0:T(8,128)S(1)}, f32[8]{0:T(128)S(1)}, f32[256,768]{1,0:T(8,128)}, s32[]{:T(128)}) %tuple.31), condition=%wide.region_2.0_spmd, body=%wide.region_0.0_spmd.sunk | while | flops 18876416 | bytes 958861 | solution.py:39
  45.1 2.2 %collective-permute-start = (f32[8,768]{1,0:T(8,128)S(1)}, f32[8,768]{1,0:T(8,128)S(1)}, u32[]{:S(2)}, u32[]{:S(2)}) collective-permute-start(f32[8,768]{1,0:T(8,128)S(1)} %copy.19), channel_id=1, source_target_pairs={{0,8},{8,16},{16,24},{24,0},{1,9},{9,17},{17,25},{25,1},{2,10},{10... | collective-permute-start | bytes 73736 | tf_op jit(solution)/shard_map/while/body/eval_jaxpr/ppermute | solution.py:13
  47.3 2.0 convolution_reduce_fusion.2
  49.3 1.4 collective-permute-start.1
  50.7 82.6 %collective-permute-done.1 = f32[8]{0:T(128)S(1)} collective-permute-done((f32[8]{0:T(128)S(1)}, f32[8]{0:T(128)S(1)}, u32[]{:S(2)}, u32[]{:S(2)}) %collective-permute-start.1) | collective-permute-done | bytes 64 | tf_op jit(solution)/shard_map/while/body/eval_jaxpr/ppermute | solution.py:13
  133.3 2.0 convolution_reduce_fusion.2
  135.3 2.1 %collective-permute-start.1 = (f32[8]{0:T(128)S(1)}, f32[8]{0:T(128)S(1)}, u32[]{:S(2)}, u32[]{:S(2)}) collective-permute-start(f32[8]{0:T(128)S(1)} %max.6), channel_id=1, source_target_pairs={{0,8},{8,16},{16,24},{24,0},{1,9},{9,17},{17,25},{25,1},{2,10},{10... | collective-permute-start | bytes 104 | tf_op jit(solution)/shard_map/while/body/eval_jaxpr/ppermute | solution.py:13
  137.4 2.3 %collective-permute-done.1 = f32[8]{0:T(128)S(1)} collective-permute-done((f32[8]{0:T(128)S(1)}, f32[8]{0:T(128)S(1)}, u32[]{:S(2)}, u32[]{:S(2)}) %collective-permute-start.1) | collective-permute-done | bytes 64 | tf_op jit(solution)/shard_map/while/body/eval_jaxpr/ppermute | solution.py:13
  139.8 1.2 collective-permute-start
  141.0 2.0 convolution_reduce_fusion.2
  142.9 1.4 collective-permute-start.1
  144.3 3.1 %collective-permute-done.1 = f32[8]{0:T(128)S(1)} collective-permute-done((f32[8]{0:T(128)S(1)}, f32[8]{0:T(128)S(1)}, u32[]{:S(2)}, u32[]{:S(2)}) %collective-permute-start.1) | collective-permute-done | bytes 64 | tf_op jit(solution)/shard_map/while/body/eval_jaxpr/ppermute | solution.py:13
  147.8 2.0 convolution_reduce_fusion.2
  149.8 2.5 %collective-permute-start.1 = (f32[8]{0:T(128)S(1)}, f32[8]{0:T(128)S(1)}, u32[]{:S(2)}, u32[]{:S(2)}) collective-permute-start(f32[8]{0:T(128)S(1)} %max.6), channel_id=1, source_target_pairs={{0,8},{8,16},{16,24},{24,0},{1,9},{9,17},{17,25},{25,1},{2,10},{10... | collective-permute-start | bytes 104 | tf_op jit(solution)/shard_map/while/body/eval_jaxpr/ppermute | solution.py:13
  152.3 2.0 collective-permute-done.1
  154.3 14.6 %all_gather.7 = f32[64,768]{1,0:T(8,128)S(1)} all-gather(f32[8,768]{1,0:T(8,128)S(1)} %copy-done.3), channel_id=1, replica_groups=mesh['group'=4,'member'=8] {'member'}, dimensions={0}, use_global_device_ids=true | all-gather | bytes 221184 | tf_op jit(solution)/shard_map/all_gather | solution.py:23
  169.0 4.9 %fusion.6 = (f32[4,1,256,768]{3,2,1,0:T(8,128)S(1)}, f32[4,1,256,768]{3,2,1,0:T(8,128)S(1)}, f32[4,1,256,768]{3,2,1,0:T(8,128)S(1)}) fusion(f32[4,3,256,768]{3,2,1,0:T(8,128)} %all-to-all-done.1), kind=kLoop, calls=%fused_computation.32 | loop fusion | bytes 18874368 | tf_op jit(solution)/shard_map/slice | solution.py:52
  173.9 3.3 %fusion = f32[64]{0:T(128)S(1)} fusion(f32[1024,768]{1,0:T(8,128)S(1)} %bitcast.26, f32[64,768]{1,0:T(8,128)S(1)} %all_gather.7, pred[1024]{0:T(1024)(128)(4,1)S(1)} %ge.44), kind=kOutput, calls=%fused_computation.8 | convolution fusion | flops 604110784 | bytes 3343616 | tf_op jit(solution)/shard_map/qd,rd->qr/dot_general | solution.py:55
  177.2 3.3 %fusion.1 = f32[64]{0:T(128)S(1)} fusion(f32[1024,768]{1,0:T(8,128)S(1)} %bitcast.25, f32[64,768]{1,0:T(8,128)S(1)} %all_gather.7, pred[1024]{0:T(1024)(128)(4,1)S(1)} %ge.46), kind=kOutput, calls=%fused_computation.9 | convolution fusion | flops 604110784 | bytes 3343616 | tf_op jit(solution)/shard_map/qd,rd->qr/dot_general | solution.py:55
  180.5 3.3 %fusion.2 = f32[64]{0:T(128)S(1)} fusion(f32[1024,768]{1,0:T(8,128)S(1)} %bitcast.24, f32[64,768]{1,0:T(8,128)S(1)} %all_gather.7, pred[1024]{0:T(1024)(128)(4,1)S(1)} %ge.48), kind=kOutput, calls=%fused_computation.10 | convolution fusion | flops 604110784 | bytes 3343616 | tf_op jit(solution)/shard_map/qd,rd->qr/dot_general | solution.py:55
  183.7 16.9 %pmax.7 = f32[3,64]{1,0:T(4,128)S(1)} all-reduce(f32[3,64]{1,0:T(4,128)S(1)} %pad_maximum_fusion), channel_id=1, replica_groups=mesh['group'=4,'member'=8] {'member'}, use_global_device_ids=true, to_apply=%region_7.8 | all-reduce | flops 192 | bytes 1536 | tf_op jit(solution)/shard_map/pmax | solution.py:61
  200.6 0.7 constant_dynamic-slice_fusion
  201.3 0.5 copy.26
  (43 shorter events, 1.1 us)
Async XLA Ops:
  0.6 8.6 %copy-start = (f32[4,256,768]{2,1,0:T(8,128)S(1)}, f32[4,256,768]{2,1,0:T(8,128)}, u32[]{:S(2)}) copy-start(f32[4,256,768]{2,1,0:T(8,128)} %param.10) | copy-start | bytes 9437188
  0.6 1.0 copy-start.1
  1.6 1.2 copy-start.2
  4.1 18.3 %all-to-all-start = ((s32[4,3,256]{2,1,0:T(4,128)}), s32[4,3,256]{2,1,0:T(4,128)S(1)}, u32[]{:S(2)}, u32[]{:S(2)}) async-start(s32[4,3,256]{2,1,0:T(4,128)} %broadcast_select_fusion.1), calls=%async_computation | async-start | bytes 32768 | tf_op jit(solution)/shard_map/all_to_all | solution.py:49
  22.3 6.0 %copy-start.5 = (f32[32,768]{1,0:T(8,128)S(1)}, f32[32,768]{1,0:T(8,128)}, u32[]{:S(2)}) copy-start(f32[32,768]{1,0:T(8,128)} %param.9) | copy-start | bytes 294916
  22.3 22.8 %copy-start.4 = (f32[8,768]{1,0:T(8,128)S(1)}, f32[8,768]{1,0:T(8,128)}, u32[]{:S(2)}) copy-start(f32[8,768]{1,0:T(8,128)} %param.8) | copy-start | bytes 73732
  22.3 146.7 %all-to-all-start.1 = ((f32[4,3,256,768]{3,2,1,0:T(8,128)}), f32[4,3,256,768]{3,2,1,0:T(8,128)}, u32[]{:S(2)}, u32[]{:S(2)}) async-start(f32[4,3,256,768]{3,2,1,0:T(8,128)} %broadcast_select_fusion), calls=%async_computation.1 | async-start | bytes 18874368 | tf_op jit(solution)/shard_map/all_to_all | solution.py:48
  28.3 126.0 %copy-start.3 = (f32[8,768]{1,0:T(8,128)S(1)}, f32[8,768]{1,0:T(8,128)}, u32[]{:S(2)}) copy-start(f32[8,768]{1,0:T(8,128)} %param.8) | copy-start | bytes 73732
  45.1 88.1 %collective-permute-start = (f32[8,768]{1,0:T(8,128)S(1)}, f32[8,768]{1,0:T(8,128)S(1)}, u32[]{:S(2)}, u32[]{:S(2)}) collective-permute-start(f32[8,768]{1,0:T(8,128)S(1)} %copy.19), channel_id=1, source_target_pairs={{0,8},{8,16},{16,24},{24,0},{1,9},{9,17},{17,25},{25,1},{2,10},{10... | collective-permute-start | bytes 73736 | tf_op jit(solution)/shard_map/while/body/eval_jaxpr/ppermute | solution.py:13
  49.3 84.0 %collective-permute-start.1 = (f32[8]{0:T(128)S(1)}, f32[8]{0:T(128)S(1)}, u32[]{:S(2)}, u32[]{:S(2)}) collective-permute-start(f32[8]{0:T(128)S(1)} %max.6), channel_id=1, source_target_pairs={{0,8},{8,16},{16,24},{24,0},{1,9},{9,17},{17,25},{25,1},{2,10},{10... | collective-permute-start | bytes 104 | tf_op jit(solution)/shard_map/while/body/eval_jaxpr/ppermute | solution.py:13
  133.3 6.5 %collective-permute-start = (f32[8,768]{1,0:T(8,128)S(1)}, f32[8,768]{1,0:T(8,128)S(1)}, u32[]{:S(2)}, u32[]{:S(2)}) collective-permute-start(f32[8,768]{1,0:T(8,128)S(1)} %copy.19), channel_id=1, source_target_pairs={{0,8},{8,16},{16,24},{24,0},{1,9},{9,17},{17,25},{25,1},{2,10},{10... | collective-permute-start | bytes 73736 | tf_op jit(solution)/shard_map/while/body/eval_jaxpr/ppermute | solution.py:13
  135.3 4.5 %collective-permute-start.1 = (f32[8]{0:T(128)S(1)}, f32[8]{0:T(128)S(1)}, u32[]{:S(2)}, u32[]{:S(2)}) collective-permute-start(f32[8]{0:T(128)S(1)} %max.6), channel_id=1, source_target_pairs={{0,8},{8,16},{16,24},{24,0},{1,9},{9,17},{17,25},{25,1},{2,10},{10... | collective-permute-start | bytes 104 | tf_op jit(solution)/shard_map/while/body/eval_jaxpr/ppermute | solution.py:13
  139.8 7.7 %collective-permute-start = (f32[8,768]{1,0:T(8,128)S(1)}, f32[8,768]{1,0:T(8,128)S(1)}, u32[]{:S(2)}, u32[]{:S(2)}) collective-permute-start(f32[8,768]{1,0:T(8,128)S(1)} %copy.19), channel_id=1, source_target_pairs={{0,8},{8,16},{16,24},{24,0},{1,9},{9,17},{17,25},{25,1},{2,10},{10... | collective-permute-start | bytes 73736 | tf_op jit(solution)/shard_map/while/body/eval_jaxpr/ppermute | solution.py:13
  142.9 4.5 %collective-permute-start.1 = (f32[8]{0:T(128)S(1)}, f32[8]{0:T(128)S(1)}, u32[]{:S(2)}, u32[]{:S(2)}) collective-permute-start(f32[8]{0:T(128)S(1)} %max.6), channel_id=1, source_target_pairs={{0,8},{8,16},{16,24},{24,0},{1,9},{9,17},{17,25},{25,1},{2,10},{10... | collective-permute-start | bytes 104 | tf_op jit(solution)/shard_map/while/body/eval_jaxpr/ppermute | solution.py:13
  147.4 6.9 %collective-permute-start = (f32[8,768]{1,0:T(8,128)S(1)}, f32[8,768]{1,0:T(8,128)S(1)}, u32[]{:S(2)}, u32[]{:S(2)}) collective-permute-start(f32[8,768]{1,0:T(8,128)S(1)} %copy.19), channel_id=1, source_target_pairs={{0,8},{8,16},{16,24},{24,0},{1,9},{9,17},{17,25},{25,1},{2,10},{10... | collective-permute-start | bytes 73736 | tf_op jit(solution)/shard_map/while/body/eval_jaxpr/ppermute | solution.py:13
  149.8 4.5 %collective-permute-start.1 = (f32[8]{0:T(128)S(1)}, f32[8]{0:T(128)S(1)}, u32[]{:S(2)}, u32[]{:S(2)}) collective-permute-start(f32[8]{0:T(128)S(1)} %max.6), channel_id=1, source_target_pairs={{0,8},{8,16},{16,24},{24,0},{1,9},{9,17},{17,25},{25,1},{2,10},{10... | collective-permute-start | bytes 104 | tf_op jit(solution)/shard_map/while/body/eval_jaxpr/ppermute | solution.py:13
where the time goes:
time: 202 us
  waiting for transfers between devices  90.1 us (45%)
  blocking collectives  48.3 us (24%)
  starting transfers between devices  22.3 us (11%)
  matrix products  17.7 us (9%)
  local copies, waits for them, and re-layouts  12.6 us (6%)
  other arithmetic  10.1 us (5%)
    ppermute x8, waiting for transfers between devices, shifted(): return lax.ppermute(value, axis, pairs)  90.1 us
    pmax x1, blocking collectives, local(): fine_all = lax.pmax(fine_partial, 'member')  16.9 us
    all_gather x1, blocking collectives, local(): group_centroids = lax.all_gather(centroids, 'member', axis=0, tiled=True)  16.8 us
    all_gather x1, blocking collectives, local(): group_block = lax.all_gather(queries, 'member', axis=0, tiled=True)  14.6 us
    ppermute x8, starting transfers between devices, shifted(): return lax.ppermute(value, axis, pairs)  11.2 us
    dot_general x3, matrix products, local(): jnp.einsum('qd,rd->qr', group_block, vectors, preferred_element_type=jnp....  9.82 us
    select_n x1, other arithmetic, local(): outgoing = jnp.take(stored, local_slot, axis=0)  8.28 us
    dot_general x4, matrix products, travel(): jnp.einsum('qd,cd->qc', query_block, group_centroids, preferred_element_t...  7.84 us
  transfers between devices with their start and end apart: 10, of which 4 were waited for; matrix products, arithmetic and copies ran while one was open for 10% of the time, Pallas kernels for 0%

commit v1 on v0

v1 whole, which is shorter than its diff:
```python
import functools

import jax
import jax.numpy as jnp
from jax import lax
from jax.experimental import pallas as pl
from jax.experimental.pallas import tpu as pltpu
from jax.sharding import PartitionSpec as P

LOWEST = -1e30
TILE = 256
NT = (((1,), (1,)), ((), ()))
VMEM_LIMIT = 48 * 2**20


def swapped(value, axis, mask):
    count = lax.axis_size(axis)
    return lax.ppermute(value, axis, [(source, source ^ mask) for source in range(count)])


def gathered(value, axis, first):
    count = lax.axis_size(axis)
    while first < count:
        radix = min(4, count // first)
        arrived = [swapped(value, axis, first * digit) for digit in range(1, radix)]
        value = jnp.concatenate([value, *arrived], axis=0)
        first *= radix
    return value


def split(value):
    high = value.astype(jnp.bfloat16)
    low = (value - high.astype(jnp.float32)).astype(jnp.bfloat16)
    return high, low


def prepare_kernel(block, home_ref, probes_ref, ids_ref, centroids_ref, stored_ref, centers_ref, vectors_ref, places_ref, counts_ref):
    lists, length, depth = stored_ref.shape
    group = lax.axis_index("group")
    for slot in range(lists):
        vectors_ref[slot, :, :depth], vectors_ref[slot, :, depth:] = split(stored_ref[slot])
    centers_ref[:, :depth], centers_ref[:, depth:] = split(centroids_ref[...])
    valid = jnp.sum((ids_ref[...] >= 0).astype(jnp.float32), axis=1, keepdims=True)
    counts_ref[...] = jnp.broadcast_to(valid, counts_ref.shape).astype(jnp.int32)
    blocks, steps, probed = probes_ref.shape
    lane_block = lax.broadcasted_iota(jnp.int32, (1, places_ref.shape[1]), 1) // block
    for step in range(steps):

        def of_block(b, row, step=step):
            place = jnp.int32(-1)
            for j in range(probed):
                slot = home_ref[probes_ref[b, step, j]]
                place = jnp.where(slot // lists == group, slot % lists, place)
            return jnp.where(lane_block == b, place, row)

        row = jnp.full(lane_block.shape, -1, jnp.int32)
        places_ref[pl.ds(step, 1), :] = lax.fori_loop(0, blocks, of_block, row)


def prepare(queries_all, list_home, probes, vector_ids, centroids, stored):
    lists, length, depth = stored.shape
    rows = lists * length + centroids.shape[0]
    smem = pl.BlockSpec(memory_space=pltpu.SMEM)
    vmem = pl.BlockSpec(memory_space=pltpu.VMEM)
    return pl.pallas_call(
        functools.partial(prepare_kernel, queries_all // probes.shape[0]),
        out_shape=(
            jax.ShapeDtypeStruct((centroids.shape[0], 2 * depth), jnp.bfloat16),
            jax.ShapeDtypeStruct((lists, length, 2 * depth), jnp.bfloat16),
            jax.ShapeDtypeStruct((probes.shape[1], queries_all), jnp.int32),
            jax.ShapeDtypeStruct((lists, 128), jnp.int32),
        ),
        in_specs=[smem, smem, vmem, vmem, vmem],
        out_specs=(vmem, vmem, vmem, vmem),
        compiler_params=pltpu.CompilerParams(vmem_limit_bytes=VMEM_LIMIT),
        cost_estimate=pl.CostEstimate(flops=6 * rows * depth, bytes_accessed=8 * rows * depth, transcendentals=0),
        name="prepare",
    )(list_home, probes, vector_ids, centroids, stored)


def score_kernel(rows_dev, own_ref, other_ref, centers_ref, vectors_ref, places_ref, counts_ref, best_ref, queries_ref, parts_ref):
    lists, length, twice = vectors_ref.shape
    depth = twice // 2
    here = lax.axis_index("group") * lax.axis_size("member") + lax.axis_index("member")
    odd = here % 2 == 1
    pairs = TILE // (2 * rows_dev)
    first = pl.program_id(0) * pairs
    for pair in range(pairs):
        start = ((first + pair) ^ (here // 2)) * rows_dev
        source = pl.ds(pl.multiple_of(start, rows_dev), rows_dev)
        own, other = own_ref[source, :], other_ref[source, :]
        at = 2 * pair * rows_dev
        queries_ref[pl.ds(at, rows_dev), :] = jnp.where(odd, other, own)
        queries_ref[pl.ds(at + rows_dev, rows_dev), :] = jnp.where(odd, own, other)
    high, low = split(queries_ref[...])
    parts_ref[:, :depth] = high
    parts_ref[:, depth:twice] = high
    parts_ref[:, twice:] = low

    def scores(vectors):
        return lax.dot_general(vectors[...], parts_ref[:, :twice], NT, preferred_element_type=jnp.float32) + lax.dot_general(
            vectors[:, :depth], parts_ref[:, twice:], NT, preferred_element_type=jnp.float32
        )

    fine = [jnp.full((1, TILE), LOWEST, jnp.float32) for _ in range(places_ref.shape[0])]
    place = lax.broadcasted_iota(jnp.int32, (length, TILE), 0)
    for slot in range(lists):
        count = jnp.concatenate([counts_ref[pl.ds(slot, 1), :]] * (TILE // 128), axis=1)
        usable = jnp.where(place < count, scores(vectors_ref.at[slot]), LOWEST)
        best = jnp.max(usable, axis=0, keepdims=True)
        for step in range(len(fine)):
            fine[step] = jnp.where(places_ref[pl.ds(step, 1), :] == slot, best, fine[step])
    coarse = jnp.max(scores(centers_ref), axis=0, keepdims=True)
    best_ref[...] = jnp.concatenate([coarse, *fine], axis=0)


def score(rows_dev, own, other, centers, vectors, places, counts):
    queries_all, depth = 2 * own.shape[0], own.shape[1]
    whole = pl.BlockSpec(memory_space=pltpu.VMEM)
    rows = vectors.shape[0] * vectors.shape[1] + centers.shape[0]
    steps = places.shape[0]
    return pl.pallas_call(
        functools.partial(score_kernel, rows_dev),
        out_shape=jax.ShapeDtypeStruct((1 + steps, queries_all), jnp.float32),
        grid=(queries_all // TILE,),
        in_specs=[whole, whole, whole, whole, pl.BlockSpec((steps, TILE), lambda i: (0, i)), whole],
        out_specs=pl.BlockSpec((1 + steps, TILE), lambda i: (0, i)),
        scratch_shapes=[pltpu.VMEM((TILE, depth), jnp.float32), pltpu.VMEM((TILE, 3 * depth), jnp.bfloat16)],
        compiler_params=pltpu.CompilerParams(vmem_limit_bytes=VMEM_LIMIT),
        cost_estimate=pl.CostEstimate(flops=6 * rows * queries_all * depth, bytes_accessed=4 * rows * depth, transcendentals=0),
        name="score",
    )(own, other, centers, vectors, places, counts)


def local(queries, centroids, stored, vector_ids, list_home, probes):
    devices = lax.axis_size("group") * lax.axis_size("member")
    rows_dev = queries.shape[0]
    ready = prepare(devices * rows_dev, list_home, probes, vector_ids, centroids, stored)
    own = gathered(gathered(queries, "member", 2), "group", 1)
    other = swapped(own, "member", 1)
    best = score(rows_dev, own, other, *ready)
    kinds = best.shape[0]
    parts = best.reshape(kinds, devices, rows_dev).transpose(1, 0, 2)
    final = jnp.max(lax.all_to_all(parts, ("group", "member"), 0, 0, tiled=True), axis=0)
    return final[0], final[1:]


def solution(mesh):
    placed = (
        P(("group", "member"), None),
        P(("group", "member"), None),
        P("group", "member", None),
        P("group", "member"),
        P(),
        P(),
    )
    return jax.shard_map(
        local,
        mesh=mesh,
        in_specs=placed,
        out_specs=(P(("group", "member")), P(None, ("group", "member"))),
        check_vma=False,
    )
```

time: 202 us -> 38.9 us (0.19)
  waiting for transfers between devices: 90.1 us -> 9.57 us
  blocking collectives: 48.3 us -> 9.15 us
  matrix products: 17.7 us -> 0 us
  starting transfers between devices: 22.3 us -> 9.24 us
  other arithmetic: 10.1 us -> 0.04 us
  local copies, waits for them, and re-layouts: 12.6 us -> 5.01 us
  Pallas kernels: 0 us -> 4.87 us
    ppermute x8 -> x7, waiting for transfers between devices: 90.1 us -> 9.57 us  [swapped(): lax.ppermute(value, axis, [(source, source ^ mask) for source in range(co...]
    all_gather x2 -> x0, blocking collectives: 31.4 us -> none  [the longest x1 16.8 us: local(): group_centroids = lax.all_gather(centroids, 'member', axis=0, tiled=True)]
    dot_general x7 -> x0, matrix products: 17.7 us -> none  [the longest x3 9.82 us: local(): jnp.einsum('qd,rd->qr', group_block, vectors, preferred_element_type=jnp....]
    pmax x1 -> x0, blocking collectives: 16.9 us -> none  [local(): fine_all = lax.pmax(fine_partial, 'member')]
    all_to_all x2 -> x0, starting transfers between devices: 11.1 us -> none  [the longest x1 5.93 us: local(): lax.all_to_all(outgoing, 'group', split_axis=0, concat_axis=0, tiled=True)]
    select_n x4 -> x0, other arithmetic: 9.81 us -> none  [the longest x1 8.28 us: local(): outgoing = jnp.take(stored, local_slot, axis=0)]
    all_to_all x0 -> x1, blocking collectives: none -> 9.15 us  [local(): lax.all_to_all(parts, ('group', 'member'), 0, 0, tiled=True)]
    gather x5 -> x0, local copies, waits for them, and re-layouts: 6.26 us -> none  [the longest x1 4.81 us: local(): outgoing = jnp.take(stored, local_slot, axis=0)]
  transfers between devices with their start and end apart: 10 -> 7, of which waited for: 4 -> 4; matrix products, arithmetic and copies ran while one was open for 10% -> 4% of each run, Pallas kernels for 0% -> 8%
where the time goes in v1:
time: 38.9 us; the launch traced here: 38.6 us
  waiting for transfers between devices  9.57 us (25%)
  starting transfers between devices  9.24 us (24%)
  blocking collectives  9.15 us (24%)
  local copies, waits for them, and re-layouts  5.01 us (13%)
  Pallas kernels  4.87 us (13%)
  between operations  0.72 us (2%)
    ppermute x7, waiting for transfers between devices, swapped(): lax.ppermute(value, axis, [(source, source ^ mask) for source in range(co...  9.57 us
    ppermute x7, starting transfers between devices, swapped(): lax.ppermute(value, axis, [(source, source ^ mask) for source in range(co...  9.24 us
    all_to_all x1, blocking collectives, local(): lax.all_to_all(parts, ('group', 'member'), 0, 0, tiled=True)  9.15 us
    unnamed x12, local copies, waits for them, and re-layouts  3.76 us
    pallas_call x1, Pallas kernels, prepare(): pl.pallas_call(functools.partial(prepare_kernel, queries_all // probes.sh...  3.13 us
    pallas_call x1, Pallas kernels, score(): pl.pallas_call(functools.partial(score_kernel, rows_dev), out_shape=jax.S...  1.74 us
  transfers between devices with their start and end apart: 7, of which 4 were waited for; matrix products, arithmetic and copies ran while one was open for 4% of the time, Pallas kernels for 8%

profile of v1, /device:TPU:0, one launch (start us, length us, event | category | flops | bytes accessed | tf_op | source)
XLA Modules:
  0.0 38.6 jit_solution(15176648228930337668)
XLA Ops:
  0.6 4.1 %collective-permute-start.1 = (f32[8,768]{1,0:T(8,128)}, f32[8,768]{1,0:T(8,128)S(1)}, u32[]{:S(2)}, u32[]{:S(2)}) collective-permute-start(f32[8,768]{1,0:T(8,128)} %param.6), channel_id=1, source_target_pairs={{0,4},{1,5},{2,6},{3,7},{4,0},{5,1},{6,2},{7,3},{8,12},{9,13},{10,... | collective-permute-start | bytes 73736 | tf_op jit(solution)/shard_map/ppermute | solution.py:18
  4.7 1.6 %collective-permute-start = (f32[8,768]{1,0:T(8,128)}, f32[8,768]{1,0:T(8,128)S(1)}, u32[]{:S(2)}, u32[]{:S(2)}) collective-permute-start(f32[8,768]{1,0:T(8,128)} %param.6), channel_id=1, source_target_pairs={{0,2},{1,3},{2,0},{3,1},{4,6},{5,7},{6,4},{7,5},{8,10},{9,11},{10,... | collective-permute-start | bytes 73736 | tf_op jit(solution)/shard_map/ppermute | solution.py:18
  6.3 0.0 collective-permute-start.2
  6.3 0.8 %constant_dynamic-update-slice_fusion.3 = (f32[32,768]{1,0:T(8,128)S(1)}, f32[128,768]{1,0:T(8,128)S(1)}) fusion(f32[8,768]{1,0:T(8,128)} %param.6), kind=kLoop, calls=%fused_computation.3 | loop fusion | bytes 73728
  7.1 1.7 %collective-permute-done = f32[8,768]{1,0:T(8,128)S(1)} collective-permute-done((f32[8,768]{1,0:T(8,128)}, f32[8,768]{1,0:T(8,128)S(1)}, u32[]{:S(2)}, u32[]{:S(2)}) %collective-permute-start) | collective-permute-done | bytes 24608 | tf_op jit(solution)/shard_map/ppermute | solution.py:18
  8.8 0.0 collective-permute-done.1
  8.8 3.3 %collective-permute-done.2 = f32[8,768]{1,0:T(8,128)S(1)} collective-permute-done((f32[8,768]{1,0:T(8,128)}, f32[8,768]{1,0:T(8,128)S(1)}, u32[]{:S(2)}, u32[]{:S(2)}) %collective-permute-start.2) | collective-permute-done | bytes 24608 | tf_op jit(solution)/shard_map/ppermute | solution.py:18
  12.1 1.5 %collective-permute-start.3 = (f32[32,768]{1,0:T(8,128)S(1)}, f32[32,768]{1,0:T(8,128)S(1)}, u32[]{:S(2)}, u32[]{:S(2)}) collective-permute-start(f32[32,768]{1,0:T(8,128)S(1)} %get-tuple-element.10), channel_id=1, source_target_pairs={{0,8},{8,0},{16,24},{24,16},{1,9},{9,1},{17,25},{25,17},{2,10},{10... | collective-permute-start | bytes 294920 | tf_op jit(solution)/shard_map/ppermute | solution.py:18
  13.6 1.5 %collective-permute-start.5 = (f32[32,768]{1,0:T(8,128)S(1)}, f32[32,768]{1,0:T(8,128)S(1)}, u32[]{:S(2)}, u32[]{:S(2)}) collective-permute-start(f32[32,768]{1,0:T(8,128)S(1)} %get-tuple-element.10), channel_id=1, source_target_pairs={{0,24},{8,16},{16,8},{24,0},{1,25},{9,17},{17,9},{25,1},{2,26},{10... | collective-permute-start | bytes 294920 | tf_op jit(solution)/shard_map/ppermute | solution.py:18
  15.1 0.5 %collective-permute-start.4 = (f32[32,768]{1,0:T(8,128)S(1)}, f32[32,768]{1,0:T(8,128)S(1)}, u32[]{:S(2)}, u32[]{:S(2)}) collective-permute-start(f32[32,768]{1,0:T(8,128)S(1)} %get-tuple-element.10), channel_id=1, source_target_pairs={{0,16},{8,24},{16,0},{24,8},{1,17},{9,25},{17,1},{25,9},{2,18},{10... | collective-permute-start | bytes 294920 | tf_op jit(solution)/shard_map/ppermute | solution.py:18
  15.6 1.6 %collective-permute-done.3 = f32[32,768]{1,0:T(8,128)S(1)} collective-permute-done((f32[32,768]{1,0:T(8,128)S(1)}, f32[32,768]{1,0:T(8,128)S(1)}, u32[]{:S(2)}, u32[]{:S(2)}) %collective-permute-start.3) | collective-permute-done | bytes 98336 | tf_op jit(solution)/shard_map/ppermute | solution.py:18
  17.2 3.0 %collective-permute-done.4 = f32[32,768]{1,0:T(8,128)S(1)} collective-permute-done((f32[32,768]{1,0:T(8,128)S(1)}, f32[32,768]{1,0:T(8,128)S(1)}, u32[]{:S(2)}, u32[]{:S(2)}) %collective-permute-start.4) | collective-permute-done | bytes 98336 | tf_op jit(solution)/shard_map/ppermute | solution.py:18
  20.2 0.0 collective-permute-done.5
  20.2 0.1 collective-permute-start.6
  20.3 0.7 %copy.10.probes_ref = s32[4,3,4]{2,1,0:T(4,128)S(1)} copy(s32[4,3,4]{2,0,1:T(4,128)} %param.11) | data formatting | bytes 384 | tf_op args[5]
  21.0 0.0 copy-start
  21.0 0.9 %copy-done = f32[32,768]{1,0:T(8,128)S(1)} copy-done((f32[32,768]{1,0:T(8,128)S(1)}, f32[32,768]{1,0:T(8,128)}, u32[]{:S(2)}) %copy-start) | copy-done | bytes 98328
  21.9 0.0 copy-start.1
  21.9 0.7 %copy-done.1 = s32[4,256]{1,0:T(4,128)S(1)} copy-done((s32[4,256]{1,0:T(4,128)S(1)}, s32[4,256]{1,0:T(4,128)}, u32[]{:S(2)}) %copy-start.1) | copy-done | bytes 4120
  22.6 0.0 copy-start.2
  22.6 0.7 %copy-done.2 = s32[16]{0:T(128)S(1)} copy-done((s32[16]{0:T(128)S(1)}, s32[16]{0:T(128)}, u32[]{:S(2)}) %copy-start.2) | copy-done | bytes 88
  23.3 3.1 %prepare.1 = (bf16[32,1536]{1,0:T(8,128)(2,1)S(1)}, bf16[4,256,1536]{2,1,0:T(8,128)(2,1)S(1)}, s32[3,256]{1,0:T(4,128)S(1)}, s32[4,128]{1,0:T(4,128)S(1)}) custom-call(s32[16]{0:T(128)S(1)} %copy-done.2, s32[4,3,4]{2,1,0:T(4,128)S(1)} %copy.10.probes_ref, s32[4,256]{1,0:T(4,128)S(1)} %copy-done.1, f32[32,768]{1,0:T(8,128)S(1)} %copy-done, ...), custom_call_target="tpu_custom_call" | custom-call | flops 4866048 | bytes 6488064 | tf_op jit(solution)/shard_map/prepare/pallas_call | solution.py:65
  26.4 0.0 collective-permute-done.6.other_ref
  26.4 1.7 %score.1 = f32[4,256]{1,0:T(4,128)S(1)} custom-call(f32[128,768]{1,0:T(8,128)S(1)} %constant_dynamic-update-slice_fusion.4.own_ref, f32[128,768]{1,0:T(8,128)S(1)} %collective-permute-done.6.other_ref, bf16[32,1536]{1,0:T(8,128)(2,1)S(1)} %get-tuple-element.6.centers_ref, bf16[4,256,1536]{2,1,0:T(8,128)(2,1)S(1)} %get-tuple-element.7.vectors_ref, ...), custom_call_target="tpu_custom_call" | custom-call | flops 1245708288 | bytes 3244032 | tf_op jit(solution)/shard_map/score/pallas_call | solution.py:122
  28.2 0.1 reshape.7
  28.3 9.2 %all_to_all.5 = f32[32,4,8]{2,1,0:T(4,128)S(1)} all-to-all(f32[32,4,8]{2,1,0:T(4,128)S(1)} %copy.11), channel_id=1, replica_groups=mesh['group'=4,'member'=8] {'group','member'}, dimensions={0} | all-to-all | bytes 8192 | tf_op jit(solution)/shard_map/all_to_all | solution.py:144
  37.5 0.5 %slice_bitcast_fusion = f32[8]{0:T(128)} fusion(f32[4,8]{1,0:T(4,128)S(1)} %reduce_max.9), kind=kLoop, calls=%fused_computation.11 | loop fusion | bytes 64 | tf_op jit(solution)/shard_map/squeeze | solution.py:145
  38.0 0.6 %slice.7 = f32[3,8]{1,0:T(4,128)} slice(f32[4,8]{1,0:T(4,128)S(1)} %reduce_max.9), slice={[1:4], [0:8]} | slice | bytes 192 | tf_op jit(solution)/shard_map/slice | solution.py:145
  (8 shorter events, 0.1 us)
Async XLA Ops:
  0.6 8.1 %collective-permute-start.1 = (f32[8,768]{1,0:T(8,128)}, f32[8,768]{1,0:T(8,128)S(1)}, u32[]{:S(2)}, u32[]{:S(2)}) collective-permute-start(f32[8,768]{1,0:T(8,128)} %param.6), channel_id=1, source_target_pairs={{0,4},{1,5},{2,6},{3,7},{4,0},{5,1},{6,2},{7,3},{8,12},{9,13},{10,... | collective-permute-start | bytes 73736 | tf_op jit(solution)/shard_map/ppermute | solution.py:18
  4.7 4.0 %collective-permute-start = (f32[8,768]{1,0:T(8,128)}, f32[8,768]{1,0:T(8,128)S(1)}, u32[]{:S(2)}, u32[]{:S(2)}) collective-permute-start(f32[8,768]{1,0:T(8,128)} %param.6), channel_id=1, source_target_pairs={{0,2},{1,3},{2,0},{3,1},{4,6},{5,7},{6,4},{7,5},{8,10},{9,11},{10,... | collective-permute-start | bytes 73736 | tf_op jit(solution)/shard_map/ppermute | solution.py:18
  6.3 5.8 %collective-permute-start.2 = (f32[8,768]{1,0:T(8,128)}, f32[8,768]{1,0:T(8,128)S(1)}, u32[]{:S(2)}, u32[]{:S(2)}) collective-permute-start(f32[8,768]{1,0:T(8,128)} %param.6), channel_id=1, source_target_pairs={{0,6},{1,7},{2,4},{3,5},{4,2},{5,3},{6,0},{7,1},{8,14},{9,15},{10,... | collective-permute-start | bytes 73736 | tf_op jit(solution)/shard_map/ppermute | solution.py:18
  12.1 5.0 %collective-permute-start.3 = (f32[32,768]{1,0:T(8,128)S(1)}, f32[32,768]{1,0:T(8,128)S(1)}, u32[]{:S(2)}, u32[]{:S(2)}) collective-permute-start(f32[32,768]{1,0:T(8,128)S(1)} %get-tuple-element.10), channel_id=1, source_target_pairs={{0,8},{8,0},{16,24},{24,16},{1,9},{9,1},{17,25},{25,17},{2,10},{10... | collective-permute-start | bytes 294920 | tf_op jit(solution)/shard_map/ppermute | solution.py:18
  13.6 6.6 %collective-permute-start.5 = (f32[32,768]{1,0:T(8,128)S(1)}, f32[32,768]{1,0:T(8,128)S(1)}, u32[]{:S(2)}, u32[]{:S(2)}) collective-permute-start(f32[32,768]{1,0:T(8,128)S(1)} %get-tuple-element.10), channel_id=1, source_target_pairs={{0,24},{8,16},{16,8},{24,0},{1,25},{9,17},{17,9},{25,1},{2,26},{10... | collective-permute-start | bytes 294920 | tf_op jit(solution)/shard_map/ppermute | solution.py:18
  15.1 5.1 %collective-permute-start.4 = (f32[32,768]{1,0:T(8,128)S(1)}, f32[32,768]{1,0:T(8,128)S(1)}, u32[]{:S(2)}, u32[]{:S(2)}) collective-permute-start(f32[32,768]{1,0:T(8,128)S(1)} %get-tuple-element.10), channel_id=1, source_target_pairs={{0,16},{8,24},{16,0},{24,8},{1,17},{9,25},{17,1},{25,9},{2,18},{10... | collective-permute-start | bytes 294920 | tf_op jit(solution)/shard_map/ppermute | solution.py:18
  20.2 6.2 %collective-permute-start.6 = (f32[128,768]{1,0:T(8,128)S(1)}, f32[128,768]{1,0:T(8,128)S(1)}, u32[]{:S(2)}, u32[]{:S(2)}) collective-permute-start(f32[128,768]{1,0:T(8,128)S(1)} %constant_dynamic-update-slice_fusion.4.own_ref), channel_id=1, source_target_pairs={{0,1},{1,0},{2,3},{3,2},{4,5},{5,4},{6,7},{7,6},{8,9},{9,8},{10,11... | collective-permute-start | bytes 1179656 | tf_op jit(solution)/shard_map/ppermute | solution.py:18
  21.0 0.9 %copy-start = (f32[32,768]{1,0:T(8,128)S(1)}, f32[32,768]{1,0:T(8,128)}, u32[]{:S(2)}) copy-start(f32[32,768]{1,0:T(8,128)} %centroids_ref.1) | copy-start | bytes 294916
  21.9 0.7 %copy-start.1 = (s32[4,256]{1,0:T(4,128)S(1)}, s32[4,256]{1,0:T(4,128)}, u32[]{:S(2)}) copy-start(s32[4,256]{1,0:T(4,128)} %ids_ref.1) | copy-start | bytes 12292
  22.6 0.7 %copy-start.2 = (s32[16]{0:T(128)S(1)}, s32[16]{0:T(128)}, u32[]{:S(2)}) copy-start(s32[16]{0:T(128)} %home_ref.1) | copy-start | bytes 196

commit v2 on v1

v2 whole, which is shorter than its diff:
```python
import functools

import jax
import jax.numpy as jnp
from jax import lax
from jax.experimental import pallas as pl
from jax.experimental.pallas import tpu as pltpu
from jax.sharding import PartitionSpec as P

LOWEST = -1e30
TILE = 128
BOTH = ("group", "member")
NT = (((1,), (1,)), ((), ()))
LARGE = 48 * 2**20
SMALL = 16 * 2**20
WHOLE = pl.BlockSpec(memory_space=pltpu.VMEM)
ANYWHERE = pl.BlockSpec(memory_space=pl.ANY)


def stages():
    members, groups = lax.axis_size("member"), lax.axis_size("group")
    inner = [1 << k for k in range(1, members.bit_length() - 1)]
    outer = [members << k for k in range(groups.bit_length() - 1)]
    listed = []
    for bits in (inner, outer):
        for at in range(0, len(bits), 2):
            low, *rest = bits[at : at + 2]
            listed.append([low | rest[0], rest[0], low] if rest else [low])
    return listed


def exchanged(value, mask):
    devices = lax.axis_size("group") * lax.axis_size("member")
    return lax.ppermute(value, BOTH, [(d, d ^ mask) for d in range(devices)])


def positions():
    offsets = [0]
    for stage in stages():
        offsets = [offset ^ mask for mask in [0, *stage] for offset in offsets]
    return [offsets.index(2 << k) for k in range(len(offsets).bit_length() - 1)]


def position(chip):
    place = 0
    for k, at in enumerate(positions()):
        place = place ^ (((chip >> k) & 1) * at)
    return place


def here():
    return lax.axis_index("group") * lax.axis_size("member") + lax.axis_index("member")


def crossed(chips):
    found = 0
    for stage in stages():
        mask = functools.reduce(lambda a, b: a | b, stage) >> 1
        found = found ^ jnp.where((chips & mask) != 0, 1, 0)
    return found


def split(value):
    high = value.astype(jnp.bfloat16)
    low = (value - high.astype(jnp.float32)).astype(jnp.bfloat16)
    return high, low


def lookup_kernel(home_hbm, probes_hbm, ids_hbm, places_ref, counts_ref, home_ref, probes_ref, ids_ref, sems, *, lists, lanes):
    copies = [
        pltpu.make_async_copy(source, target, sems.at[k])
        for k, (source, target) in enumerate([(home_hbm, home_ref), (probes_hbm, probes_ref), (ids_hbm, ids_ref)])
    ]
    for copy in copies:
        copy.start()
    for copy in copies:
        copy.wait()
    group = lax.axis_index("group")
    valid = jnp.sum((ids_ref[...] >= 0).astype(jnp.float32), axis=1, keepdims=True)
    counts_ref[...] = jnp.broadcast_to(valid, counts_ref.shape).astype(jnp.int32)
    steps, blocks, probed = probes_ref.shape
    lane_block = lax.broadcasted_iota(jnp.int32, (1, places_ref.shape[1]), 1) // lanes
    for step in range(steps):

        def of_block(b, row, step=step):
            place = jnp.int32(-1)
            for j in range(probed):
                slot = home_ref[probes_ref[step, b, j]]
                place = jnp.where(slot // lists == group, slot % lists, place)
            return jnp.where(lane_block == b, place, row)

        row = jnp.full(lane_block.shape, -1, jnp.int32)
        places_ref[pl.ds(step, 1), :] = lax.fori_loop(0, blocks, of_block, row)


def lookup(half, list_home, probes, vector_ids):
    steps, blocks, _ = probes.shape
    lists = vector_ids.shape[0]
    return pl.pallas_call(
        functools.partial(lookup_kernel, lists=lists, lanes=half // blocks),
        out_shape=(
            jax.ShapeDtypeStruct((steps, half), jnp.int32),
            jax.ShapeDtypeStruct((lists, TILE), jnp.int32),
        ),
        in_specs=[ANYWHERE] * 3,
        out_specs=(WHOLE, WHOLE),
        scratch_shapes=[
            pltpu.SMEM(list_home.shape, jnp.int32),
            pltpu.SMEM(probes.shape, jnp.int32),
            pltpu.VMEM(vector_ids.shape, jnp.int32),
            pltpu.SemaphoreType.DMA((3,)),
        ],
        compiler_params=pltpu.CompilerParams(vmem_limit_bytes=SMALL),
        cost_estimate=pl.CostEstimate(flops=10000, bytes_accessed=100000, transcendentals=0),
        name="lookup",
    )(list_home, probes, vector_ids)


def prepare_kernel(centroids_hbm, stored_hbm, centers_ref, vectors_ref, centroids_ref, stored_ref, sems):
    lists, length, _ = stored_ref.shape
    count = centroids_ref.shape[0]
    copies = [pltpu.make_async_copy(stored_hbm.at[k], stored_ref.at[k], sems.at[k]) for k in range(lists)]
    copies.append(pltpu.make_async_copy(centroids_hbm, centroids_ref, sems.at[lists]))
    for copy in copies:
        copy.start()
    for k in range(lists):
        copies[k].wait()
        vectors_ref[k, :length], vectors_ref[k, length:] = split(stored_ref[k])
    copies[lists].wait()
    centers_ref[:count], centers_ref[count:] = split(centroids_ref[...])


def prepare(centroids, stored):
    lists, length, depth = stored.shape
    rows = lists * length + centroids.shape[0]
    return pl.pallas_call(
        prepare_kernel,
        out_shape=(
            jax.ShapeDtypeStruct((2 * centroids.shape[0], depth), jnp.bfloat16),
            jax.ShapeDtypeStruct((lists, 2 * length, depth), jnp.bfloat16),
        ),
        in_specs=[ANYWHERE] * 2,
        out_specs=(WHOLE, WHOLE),
        scratch_shapes=[
            pltpu.VMEM(centroids.shape, jnp.float32),
            pltpu.VMEM(stored.shape, jnp.float32),
            pltpu.SemaphoreType.DMA((lists + 1,)),
        ],
        compiler_params=pltpu.CompilerParams(vmem_limit_bytes=LARGE),
        cost_estimate=pl.CostEstimate(flops=6 * rows * depth, bytes_accessed=8 * rows * depth, transcendentals=0),
        name="prepare",
    )(centroids, stored)


def best_scores(rows_dev, blocks_ref, centers_ref, vectors_ref, places_ref, counts_ref, queries_ref, parts_ref):
    lists, length = vectors_ref.shape[0], vectors_ref.shape[1] // 2
    origin = position(here() >> 1)
    chunks = TILE // rows_dev
    for chunk in range(chunks):
        offset = position(chunk if blocks_ref.shape[0] == TILE else pl.program_id(0) * chunks + chunk)
        source = pl.multiple_of((origin ^ offset) * rows_dev, rows_dev)
        queries_ref[pl.ds(chunk * rows_dev, rows_dev), :] = blocks_ref[pl.ds(source, rows_dev), :]
    parts_ref[:TILE], parts_ref[TILE:] = split(queries_ref[...])

    def scores(vectors):
        count = vectors.shape[0] // 2
        terms = lax.dot_general(vectors[...], parts_ref[...], NT, preferred_element_type=jnp.float32)
        small = terms[:count, TILE:] + (terms[count:, :TILE] + terms[count:, TILE:])
        return terms[:count, :TILE] + small

    fine = [jnp.full((1, TILE), LOWEST, jnp.float32) for _ in range(places_ref.shape[0])]
    place = lax.broadcasted_iota(jnp.int32, (length, TILE), 0)
    for slot in range(lists):
        usable = jnp.where(place < counts_ref[pl.ds(slot, 1), :], scores(vectors_ref.at[slot]), LOWEST)
        best = jnp.max(usable, axis=0, keepdims=True)
        for step in range(len(fine)):
            fine[step] = jnp.where(places_ref[pl.ds(step, 1), :] == slot, best, fine[step])
    coarse = jnp.max(scores(centers_ref), axis=0, keepdims=True)
    return jnp.concatenate([coarse, *fine], axis=0)


def own_kernel(*refs, rows_dev):
    *ins, best_ref, queries_ref, parts_ref = refs
    best_ref[0] = best_scores(rows_dev, *ins, queries_ref, parts_ref)


def other_kernel(own_ref, *refs, rows_dev):
    *ins, out_ref, queries_ref, parts_ref = refs
    own, other = own_ref[0], best_scores(rows_dev, *ins, queries_ref, parts_ref)
    chips = out_ref.shape[0] // 2
    for chip in range(chips):
        straight = crossed((pl.program_id(0) * chips + chip) ^ (here() >> 1)) == (here() & 1)
        out_ref[2 * chip] = jnp.where(straight, own, other)
        out_ref[2 * chip + 1] = jnp.where(straight, other, own)


def score(rows_dev, kernel, blocks, centers, vectors, places, counts, own=None):
    half, depth = blocks.shape
    rows = vectors.shape[0] * vectors.shape[1] // 2 + centers.shape[0] // 2
    kinds = 1 + places.shape[0]
    per = pl.BlockSpec((1, kinds, TILE), lambda i: (i, 0, 0))
    devices = 2 * TILE // rows_dev
    return pl.pallas_call(
        functools.partial(kernel, rows_dev=rows_dev),
        out_shape=jax.ShapeDtypeStruct((half // TILE * (1 if own is None else devices), kinds, TILE), jnp.float32),
        grid=(half // TILE,),
        in_specs=[*([] if own is None else [per]), WHOLE, WHOLE, WHOLE, pl.BlockSpec((kinds - 1, TILE), lambda i: (0, i)), WHOLE],
        out_specs=per if own is None else pl.BlockSpec((devices, kinds, TILE), lambda i: (i, 0, 0)),
        scratch_shapes=[pltpu.VMEM((TILE, depth), jnp.float32), pltpu.VMEM((2 * TILE, depth), jnp.bfloat16)],
        compiler_params=pltpu.CompilerParams(vmem_limit_bytes=LARGE),
        cost_estimate=pl.CostEstimate(flops=8 * rows * half * depth, bytes_accessed=4 * rows * depth, transcendentals=0),
        name=kernel.__name__,
    )(*([] if own is None else [own]), blocks, centers, vectors, places, counts)


def finish_kernel(arrived_ref, coarse_ref, fine_ref, *, rows_dev):
    best = jnp.max(arrived_ref[...], axis=0)
    lane = ((here() >> 1) * rows_dev) % TILE
    best = pltpu.roll(best, (TILE - lane) % TILE, 1)
    coarse_ref[...] = best[0, :rows_dev]
    fine_ref[...] = best[1:, :rows_dev]


def finish(rows_dev, arrived):
    kinds = arrived.shape[1]
    return pl.pallas_call(
        functools.partial(finish_kernel, rows_dev=rows_dev),
        out_shape=(
            jax.ShapeDtypeStruct((rows_dev,), jnp.float32),
            jax.ShapeDtypeStruct((kinds - 1, rows_dev), jnp.float32),
        ),
        in_specs=[WHOLE],
        out_specs=(WHOLE, WHOLE),
        compiler_params=pltpu.CompilerParams(vmem_limit_bytes=SMALL),
        name="finish",
    )(arrived)


def gathered(blocks, stage):
    return jnp.concatenate([blocks, *[exchanged(blocks, mask | 1) for mask in stage]], axis=0)


def local(queries, centroids, stored, vector_ids, list_home, probes):
    devices = lax.axis_size("group") * lax.axis_size("member")
    rows_dev = queries.shape[0]
    found = lookup(devices // 2 * rows_dev, list_home, probes.transpose(1, 0, 2), vector_ids)
    blocks = queries
    *early, last = stages()
    for stage in early:
        blocks = gathered(blocks, stage)
    blocks, centroids, stored, *found = lax.optimization_barrier((blocks, centroids, stored, *found))
    blocks, *split_vectors = lax.optimization_barrier((gathered(blocks, last), *prepare(centroids, stored)))
    ready = (*split_vectors, *found)
    theirs = exchanged(blocks, 1)
    own = score(rows_dev, own_kernel, blocks, *ready)
    parts = score(rows_dev, other_kernel, theirs, *ready, own=own)
    return finish(rows_dev, lax.all_to_all(parts, BOTH, 0, 0, tiled=True))


def solution(mesh):
    placed = (
        P(BOTH, None),
        P(BOTH, None),
        P("group", "member", None),
        P("group", "member"),
        P(),
        P(),
    )
    return jax.shard_map(
        local,
        mesh=mesh,
        in_specs=placed,
        out_specs=(P(BOTH), P(None, BOTH)),
        check_vma=False,
    )
```

time: 38.9 us -> 34.4 us (0.88)
  waiting for transfers between devices: 9.57 us -> 2.86 us
  blocking collectives: 9.15 us -> 11.8 us
  local copies, waits for them, and re-layouts: 5.01 us -> 2.92 us
  Pallas kernels: 4.87 us -> 6.04 us
  other arithmetic: 0.04 us -> 0.77 us
    ppermute x7, waiting for transfers between devices: 9.57 us -> 2.86 us  [exchanged(): return lax.ppermute(value, BOTH, [(d, d ^ mask) for d in range(devices)])]
    all_to_all x1, blocking collectives: 9.15 us -> 11.8 us  [local(): return finish(rows_dev, lax.all_to_all(parts, BOTH, 0, 0, tiled=True))]
    pallas_call x2 -> x5, Pallas kernels: 4.87 us -> 6.04 us  [the longest x2 2.27 us: score(): pl.pallas_call(functools.partial(kernel, rows_dev=rows_dev), out_shape=ja...]
    unnamed x12 -> x8, local copies, waits for them, and re-layouts: 3.76 us -> 2.92 us
    concatenate x0 -> x2, other arithmetic: none -> 0.77 us  [gathered(): jnp.concatenate([blocks, *[exchanged(blocks, mask | 1) for mask in stage]...]
    slice x1 -> x0, local copies, waits for them, and re-layouts: 0.58 us -> none  [local(): return (final[0], final[1:])]
    squeeze x1 -> x0, local copies, waits for them, and re-layouts: 0.51 us -> none  [local(): return (final[0], final[1:])]
  transfers between devices with their start and end apart: 7 -> 7, of which waited for: 4 -> 3; matrix products, arithmetic and copies ran while one was open for 4% -> 0% of each run, Pallas kernels for 8% -> 12%
where the time goes in v2:
time: 34.4 us; the launch traced here: 34.1 us
  blocking collectives  11.8 us (34%)
  starting transfers between devices  8.94 us (26%)
  Pallas kernels  6.04 us (18%)
  local copies, waits for them, and re-layouts  2.92 us (8%)
  waiting for transfers between devices  2.86 us (8%)
  other arithmetic  0.77 us (2%)
  between operations  0.69 us (2%)
    all_to_all x1, blocking collectives, local(): return finish(rows_dev, lax.all_to_all(parts, BOTH, 0, 0, tiled=True))  11.8 us
    ppermute x7, starting transfers between devices, exchanged(): return lax.ppermute(value, BOTH, [(d, d ^ mask) for d in range(devices)])  8.94 us
    unnamed x8, local copies, waits for them, and re-layouts  2.92 us
    ppermute x7, waiting for transfers between devices, exchanged(): return lax.ppermute(value, BOTH, [(d, d ^ mask) for d in range(devices)])  2.86 us
    pallas_call x2, Pallas kernels, score(): pl.pallas_call(functools.partial(kernel, rows_dev=rows_dev), out_shape=ja...  2.27 us
    pallas_call x1, Pallas kernels, prepare(): pl.pallas_call(prepare_kernel, out_shape=(jax.ShapeDtypeStruct((2 * centr...  2.04 us
    pallas_call x1, Pallas kernels, lookup(): pl.pallas_call(functools.partial(lookup_kernel, lists=lists, lanes=half /...  1.07 us
    concatenate x2, other arithmetic, gathered(): jnp.concatenate([blocks, *[exchanged(blocks, mask | 1) for mask in stage]...  0.77 us
  transfers between devices with their start and end apart: 7, of which 3 were waited for; matrix products, arithmetic and copies ran while one was open for 0% of the time, Pallas kernels for 12%

profile of v2, /device:TPU:0, one launch (start us, length us, event | category | flops | bytes accessed | tf_op | source)
XLA Modules:
  0.0 34.1 jit_solution(2326194556101855835)
XLA Ops:
  0.6 4.6 %collective-permute-start = (f32[8,768]{1,0:T(8,128)}, f32[8,768]{1,0:T(8,128)S(1)}, u32[]{:S(2)}, u32[]{:S(2)}) collective-permute-start(f32[8,768]{1,0:T(8,128)} %param.6), channel_id=1, source_target_pairs={{0,7},{1,6},{2,5},{3,4},{4,3},{5,2},{6,1},{7,0},{8,15},{9,14},{10,... | collective-permute-start | bytes 73736 | tf_op jit(solution)/shard_map/ppermute | solution.py:34
  5.2 0.0 collective-permute-start.1
  5.2 0.9 %collective-permute-start.2 = (f32[8,768]{1,0:T(8,128)}, f32[8,768]{1,0:T(8,128)S(1)}, u32[]{:S(2)}, u32[]{:S(2)}) collective-permute-start(f32[8,768]{1,0:T(8,128)} %param.6), channel_id=1, source_target_pairs={{0,3},{1,2},{2,1},{3,0},{4,7},{5,6},{6,5},{7,4},{8,11},{9,10},{10,... | collective-permute-start | bytes 73736 | tf_op jit(solution)/shard_map/ppermute | solution.py:34
  6.1 0.0 copy-start.1
  6.1 0.7 %copy-done.1 = s32[4,3,4]{2,0,1:T(4,128)S(1)} copy-done((s32[4,3,4]{2,0,1:T(4,128)S(1)}, s32[4,3,4]{2,0,1:T(4,128)}, u32[]{:S(2)}) %copy-start.1) | copy-done | bytes 216
  6.8 0.0 copy-start.2
  6.8 0.7 %copy-done.2 = s32[4,256]{1,0:T(4,128)S(1)} copy-done((s32[4,256]{1,0:T(4,128)S(1)}, s32[4,256]{1,0:T(4,128)}, u32[]{:S(2)}) %copy-start.2) | copy-done | bytes 4120
  7.5 0.0 copy-start.3
  7.5 0.7 %copy-done.3 = s32[16]{0:T(128)S(1)} copy-done((s32[16]{0:T(128)S(1)}, s32[16]{0:T(128)}, u32[]{:S(2)}) %copy-start.3) | copy-done | bytes 88
  8.1 1.1 %lookup.1 = (s32[3,128]{1,0:T(4,128)S(1)}, s32[4,128]{1,0:T(4,128)S(1)}) custom-call(s32[16]{0:T(128)S(1)} %copy-done.3, s32[3,4,4]{2,1,0:T(4,128)S(1)} %bitcast.1, s32[4,256]{1,0:T(4,128)S(1)} %copy-done.2), custom_call_target="tpu_custom_call" | custom-call | flops 10000 | bytes 100000 | tf_op jit(solution)/shard_map/lookup/pallas_call | solution.py:99
  9.2 0.0 collective-permute-done
  9.2 0.5 %collective-permute-done.1 = f32[8,768]{1,0:T(8,128)S(1)} collective-permute-done((f32[8,768]{1,0:T(8,128)}, f32[8,768]{1,0:T(8,128)S(1)}, u32[]{:S(2)}, u32[]{:S(2)}) %collective-permute-start.1) | collective-permute-done | bytes 24608 | tf_op jit(solution)/shard_map/ppermute | solution.py:34
  9.8 0.0 collective-permute-done.2
  9.8 0.7 %pad_maximum_fusion.1 = f32[32,768]{1,0:T(8,128)S(1)} fusion(f32[8,768]{1,0:T(8,128)S(1)} %collective-permute-done.2, f32[8,768]{1,0:T(8,128)S(1)} %collective-permute-done.1, f32[8,768]{1,0:T(8,128)S(1)} %collective-permute-done, f32[8,768]{1,0:T(8,128)} %param.6), kind=kLoop, calls=%fused_computation.1 | loop fusion | flops 73728 | bytes 196608 | tf_op jit(solution)/shard_map/concatenate | solution.py:240
  10.5 2.5 %collective-permute-start.3 = (f32[32,768]{1,0:T(8,128)S(1)}, f32[32,768]{1,0:T(8,128)S(1)}, u32[]{:S(2)}, u32[]{:S(2)}) collective-permute-start(f32[32,768]{1,0:T(8,128)S(1)} %pad_maximum_fusion.1), channel_id=1, source_target_pairs={{0,25},{1,24},{2,27},{3,26},{4,29},{5,28},{6,31},{7,30},{8,17},{9,... | collective-permute-start | bytes 294920 | tf_op jit(solution)/shard_map/ppermute | solution.py:34
  13.0 0.2 collective-permute-start.4
  13.2 0.6 %collective-permute-start.5 = (f32[32,768]{1,0:T(8,128)S(1)}, f32[32,768]{1,0:T(8,128)S(1)}, u32[]{:S(2)}, u32[]{:S(2)}) collective-permute-start(f32[32,768]{1,0:T(8,128)S(1)} %pad_maximum_fusion.1), channel_id=1, source_target_pairs={{0,9},{1,8},{2,11},{3,10},{4,13},{5,12},{6,15},{7,14},{8,1},{9,0},... | collective-permute-start | bytes 294920 | tf_op jit(solution)/shard_map/ppermute | solution.py:34
  13.8 0.0 copy-start
  13.8 0.9 %copy-done = f32[32,768]{1,0:T(8,128)S(1)} copy-done((f32[32,768]{1,0:T(8,128)S(1)}, f32[32,768]{1,0:T(8,128)}, u32[]{:S(2)}) %copy-start) | copy-done | bytes 98328
  14.7 2.0 %prepare.1 = (bf16[64,768]{1,0:T(8,128)(2,1)S(1)}, bf16[4,512,768]{2,1,0:T(8,128)(2,1)S(1)}) custom-call(f32[32,768]{1,0:T(8,128)S(1)} %copy-done, f32[4,256,768]{2,1,0:T(8,128)} %stored_hbm), custom_call_target="tpu_custom_call" | custom-call | flops 4866048 | bytes 6488064 | tf_op jit(solution)/shard_map/prepare/pallas_call | solution.py:136
  16.7 0.0 collective-permute-done.3
  16.7 1.9 %collective-permute-done.4 = f32[32,768]{1,0:T(8,128)S(1)} collective-permute-done((f32[32,768]{1,0:T(8,128)S(1)}, f32[32,768]{1,0:T(8,128)S(1)}, u32[]{:S(2)}, u32[]{:S(2)}) %collective-permute-start.4) | collective-permute-done | bytes 98336 | tf_op jit(solution)/shard_map/ppermute | solution.py:34
  18.6 0.0 collective-permute-done.5
  18.6 0.2 collective-permute-start.6
  18.8 1.1 %own_kernel.1.own_ref = f32[1,4,128]{2,1,0:T(4,128)S(1)} custom-call(f32[128,768]{1,0:T(8,128)S(1)} %pad_maximum_fusion.refs_0_, bf16[64,768]{1,0:T(8,128)(2,1)S(1)} %get-tuple-element.22.refs_1_, bf16[4,512,768]{2,1,0:T(8,128)(2,1)S(1)} %get-tuple-element.23.refs_2_, s32[3,128]{1,0:T(4,128)S(1)} %get-tuple-element.24.refs_3_, ...), custom_call_target="tpu_custom_call" | custom-call | flops 830472192 | bytes 3244032 | tf_op jit(solution)/shard_map/own_kernel/pallas_call | solution.py:203
  19.9 0.5 %collective-permute-done.6.refs_0_ = f32[128,768]{1,0:T(8,128)S(1)} collective-permute-done((f32[128,768]{1,0:T(8,128)S(1)}, f32[128,768]{1,0:T(8,128)S(1)}, u32[]{:S(2)}, u32[]{:S(2)}) %collective-permute-start.6) | collective-permute-done | bytes 393248 | tf_op jit(solution)/shard_map/ppermute | solution.py:34
  20.4 1.1 %other_kernel.1 = f32[32,4,128]{2,1,0:T(4,128)S(1)} custom-call(f32[1,4,128]{2,1,0:T(4,128)S(1)} %own_kernel.1.own_ref, f32[128,768]{1,0:T(8,128)S(1)} %collective-permute-done.6.refs_0_, bf16[64,768]{1,0:T(8,128)(2,1)S(1)} %get-tuple-element.22.refs_1_, bf16[4,512,768]{2,1,0:T(8,128)(2,1)S(1)} %get-tuple-element.23.refs_2_, ...), custom_call_target="tpu_custom_call" | custom-call | flops 830472192 | bytes 3244032 | tf_op jit(solution)/shard_map/other_kernel/pallas_call | solution.py:203
  21.6 11.8 %all_to_all.5.arrived_ref = f32[32,4,128]{2,1,0:T(4,128)S(1)} all-to-all(f32[32,4,128]{2,1,0:T(4,128)S(1)} %other_kernel.1), channel_id=1, replica_groups=mesh['group'=4,'member'=8] {'group','member'}, dimensions={0} | all-to-all | bytes 131072 | tf_op jit(solution)/shard_map/all_to_all | solution.py:257
  33.4 0.7 %finish.1 = (f32[8]{0:T(128)}, f32[3,8]{1,0:T(4,128)}) custom-call(f32[32,4,128]{2,1,0:T(4,128)S(1)} %all_to_all.5.arrived_ref), custom_call_target="tpu_custom_call" | custom-call | tf_op jit(solution)/shard_map/finish/pallas_call | solution.py:226
  (1 shorter events, 0.0 us)
Async XLA Ops:
  0.6 8.6 %collective-permute-start = (f32[8,768]{1,0:T(8,128)}, f32[8,768]{1,0:T(8,128)S(1)}, u32[]{:S(2)}, u32[]{:S(2)}) collective-permute-start(f32[8,768]{1,0:T(8,128)} %param.6), channel_id=1, source_target_pairs={{0,7},{1,6},{2,5},{3,4},{4,3},{5,2},{6,1},{7,0},{8,15},{9,14},{10,... | collective-permute-start | bytes 73736 | tf_op jit(solution)/shard_map/ppermute | solution.py:34
  5.2 4.6 %collective-permute-start.1 = (f32[8,768]{1,0:T(8,128)}, f32[8,768]{1,0:T(8,128)S(1)}, u32[]{:S(2)}, u32[]{:S(2)}) collective-permute-start(f32[8,768]{1,0:T(8,128)} %param.6), channel_id=1, source_target_pairs={{0,5},{1,4},{2,7},{3,6},{4,1},{5,0},{6,3},{7,2},{8,13},{9,12},{10,... | collective-permute-start | bytes 73736 | tf_op jit(solution)/shard_map/ppermute | solution.py:34
  5.2 4.6 %collective-permute-start.2 = (f32[8,768]{1,0:T(8,128)}, f32[8,768]{1,0:T(8,128)S(1)}, u32[]{:S(2)}, u32[]{:S(2)}) collective-permute-start(f32[8,768]{1,0:T(8,128)} %param.6), channel_id=1, source_target_pairs={{0,3},{1,2},{2,1},{3,0},{4,7},{5,6},{6,5},{7,4},{8,11},{9,10},{10,... | collective-permute-start | bytes 73736 | tf_op jit(solution)/shard_map/ppermute | solution.py:34
  6.1 0.7 %copy-start.1 = (s32[4,3,4]{2,0,1:T(4,128)S(1)}, s32[4,3,4]{2,0,1:T(4,128)}, u32[]{:S(2)}) copy-start(s32[4,3,4]{2,0,1:T(4,128)} %param.11) | copy-start | bytes 580
  6.8 0.7 %copy-start.2 = (s32[4,256]{1,0:T(4,128)S(1)}, s32[4,256]{1,0:T(4,128)}, u32[]{:S(2)}) copy-start(s32[4,256]{1,0:T(4,128)} %ids_hbm.1) | copy-start | bytes 12292
  7.5 0.7 %copy-start.3 = (s32[16]{0:T(128)S(1)}, s32[16]{0:T(128)}, u32[]{:S(2)}) copy-start(s32[16]{0:T(128)} %home_hbm.1) | copy-start | bytes 196
  10.5 6.2 %collective-permute-start.3 = (f32[32,768]{1,0:T(8,128)S(1)}, f32[32,768]{1,0:T(8,128)S(1)}, u32[]{:S(2)}, u32[]{:S(2)}) collective-permute-start(f32[32,768]{1,0:T(8,128)S(1)} %pad_maximum_fusion.1), channel_id=1, source_target_pairs={{0,25},{1,24},{2,27},{3,26},{4,29},{5,28},{6,31},{7,30},{8,17},{9,... | collective-permute-start | bytes 294920 | tf_op jit(solution)/shard_map/ppermute | solution.py:34
  13.0 5.6 %collective-permute-start.4 = (f32[32,768]{1,0:T(8,128)S(1)}, f32[32,768]{1,0:T(8,128)S(1)}, u32[]{:S(2)}, u32[]{:S(2)}) collective-permute-start(f32[32,768]{1,0:T(8,128)S(1)} %pad_maximum_fusion.1), channel_id=1, source_target_pairs={{0,17},{1,16},{2,19},{3,18},{4,21},{5,20},{6,23},{7,22},{8,25},{9,... | collective-permute-start | bytes 294920 | tf_op jit(solution)/shard_map/ppermute | solution.py:34
  13.2 5.4 %collective-permute-start.5 = (f32[32,768]{1,0:T(8,128)S(1)}, f32[32,768]{1,0:T(8,128)S(1)}, u32[]{:S(2)}, u32[]{:S(2)}) collective-permute-start(f32[32,768]{1,0:T(8,128)S(1)} %pad_maximum_fusion.1), channel_id=1, source_target_pairs={{0,9},{1,8},{2,11},{3,10},{4,13},{5,12},{6,15},{7,14},{8,1},{9,0},... | collective-permute-start | bytes 294920 | tf_op jit(solution)/shard_map/ppermute | solution.py:34
  13.8 0.9 %copy-start = (f32[32,768]{1,0:T(8,128)S(1)}, f32[32,768]{1,0:T(8,128)}, u32[]{:S(2)}) copy-start(f32[32,768]{1,0:T(8,128)} %centroids_hbm) | copy-start | bytes 294916
  18.6 1.8 %collective-permute-start.6 = (f32[128,768]{1,0:T(8,128)S(1)}, f32[128,768]{1,0:T(8,128)S(1)}, u32[]{:S(2)}, u32[]{:S(2)}) collective-permute-start(f32[128,768]{1,0:T(8,128)S(1)} %pad_maximum_fusion.refs_0_), channel_id=1, source_target_pairs={{0,1},{1,0},{2,3},{3,2},{4,5},{5,4},{6,7},{7,6},{8,9},{9,8},{10,11... | collective-permute-start | bytes 1179656 | tf_op jit(solution)/shard_map/ppermute | solution.py:34

commit v3 on v2

v3 whole, which is shorter than its diff:
```python
import functools

import jax
import jax.numpy as jnp
from jax import lax
from jax.experimental import pallas as pl
from jax.experimental.pallas import tpu as pltpu
from jax.sharding import PartitionSpec as P

LOWEST = -1e30
TILE = 128
BOTH = ("group", "member")
NT = (((1,), (1,)), ((), ()))
LARGE = 20 * 2**20
SMALL = 10 * 2**20
WHOLE = pl.BlockSpec(memory_space=pltpu.VMEM)
ANYWHERE = pl.BlockSpec(memory_space=pl.ANY)


def stages():
    members, groups = lax.axis_size("member"), lax.axis_size("group")
    inner = [1 << k for k in range(1, members.bit_length() - 1)]
    outer = [members << k for k in range(groups.bit_length() - 1)]
    listed = []
    for bits in (inner, outer):
        for at in range(0, len(bits), 2):
            low, *rest = bits[at : at + 2]
            listed.append([low | rest[0], rest[0], low] if rest else [low])
    return listed


def exchanged(value, mask):
    devices = lax.axis_size("group") * lax.axis_size("member")
    return lax.ppermute(value, BOTH, [(d, d ^ mask) for d in range(devices)])


def positions():
    offsets = [0]
    for stage in stages():
        offsets = [offset ^ mask for mask in [0, *stage] for offset in offsets]
    return [offsets.index(2 << k) for k in range(len(offsets).bit_length() - 1)]


def position(chip):
    place = 0
    for k, at in enumerate(positions()):
        place = place ^ (((chip >> k) & 1) * at)
    return place


def here():
    return lax.axis_index("group") * lax.axis_size("member") + lax.axis_index("member")


def crossed(chips):
    found = 0
    for stage in stages():
        mask = functools.reduce(lambda a, b: a | b, stage) >> 1
        found = found ^ jnp.where((chips & mask) != 0, 1, 0)
    return found


def split(value):
    high = value.astype(jnp.bfloat16)
    low = (value - high.astype(jnp.float32)).astype(jnp.bfloat16)
    return high, low


def copy_all(pairs, sems):
    copies = [pltpu.make_async_copy(source, target, sems.at[k]) for k, (source, target) in enumerate(pairs)]
    for copy in copies:
        copy.start()
    return copies


def lookup_kernel(home_hbm, probes_hbm, ids_hbm, theirs_hbm, places_ref, counts_ref, home_ref, probes_ref, ids_ref, sems, *, lanes):
    lists = ids_ref.shape[1]
    pairs = [(home_hbm, home_ref), (probes_hbm, probes_ref), (ids_hbm, ids_ref.at[0]), (theirs_hbm, ids_ref.at[1])]
    for copy in copy_all(pairs, sems):
        copy.wait()
    group = lax.axis_index("group")
    valid = jnp.sum((ids_ref[...] >= 0).astype(jnp.float32), axis=2, keepdims=True)
    counts_ref[...] = jnp.broadcast_to(valid, counts_ref.shape).astype(jnp.int32)
    steps, blocks, probed = probes_ref.shape
    lane_block = lax.broadcasted_iota(jnp.int32, (1, places_ref.shape[1]), 1) // lanes
    for step in range(steps):

        def of_block(b, row, step=step):
            place = jnp.int32(-1)
            for j in range(probed):
                slot = home_ref[probes_ref[step, b, j]]
                place = jnp.where(slot // lists == group, slot % lists, place)
            return jnp.where(lane_block == b, place, row)

        row = jnp.full(lane_block.shape, -1, jnp.int32)
        places_ref[pl.ds(step, 1), :] = lax.fori_loop(0, blocks, of_block, row)


def lookup(half, list_home, probes, vector_ids, theirs):
    steps, blocks, _ = probes.shape
    lists = vector_ids.shape[0]
    return pl.pallas_call(
        functools.partial(lookup_kernel, lanes=half // blocks),
        out_shape=(
            jax.ShapeDtypeStruct((steps, half), jnp.int32),
            jax.ShapeDtypeStruct((2, lists, TILE), jnp.int32),
        ),
        in_specs=[ANYWHERE] * 4,
        out_specs=(WHOLE, WHOLE),
        scratch_shapes=[
            pltpu.SMEM(list_home.shape, jnp.int32),
            pltpu.SMEM(probes.shape, jnp.int32),
            pltpu.VMEM((2, *vector_ids.shape), jnp.int32),
            pltpu.SemaphoreType.DMA((4,)),
        ],
        compiler_params=pltpu.CompilerParams(vmem_limit_bytes=SMALL),
        cost_estimate=pl.CostEstimate(flops=10000, bytes_accessed=100000, transcendentals=0),
        name="lookup",
    )(list_home, probes, vector_ids, theirs)


def split_kernel(centroids_hbm, stored_hbm, *refs):
    *passed, centroids_ref, stored_ref, sems = refs
    if len(passed) == 4:
        queries_hbm, centers_ref, vectors_ref, queries_ref = passed
        extra = [(queries_hbm, queries_ref)]
    else:
        centers_ref, vectors_ref = passed
        extra = []
    lists, length, _ = stored_ref.shape
    count = centroids_ref.shape[0]
    pairs = [(centroids_hbm, centroids_ref), *extra, *[(stored_hbm.at[k], stored_ref.at[k]) for k in range(lists)]]
    copies = copy_all(pairs, sems)
    for copy in copies[:-lists]:
        copy.wait()
    centers_ref[:count], centers_ref[count:] = split(centroids_ref[...])
    for k in range(lists):
        copies[k - lists].wait()
        vectors_ref[k, :length], vectors_ref[k, length:] = split(stored_ref[k])


def prepare(centroids, stored, *queries):
    lists, length, depth = stored.shape
    rows = lists * length + centroids.shape[0]
    return pl.pallas_call(
        split_kernel,
        out_shape=(
            jax.ShapeDtypeStruct((2 * centroids.shape[0], depth), jnp.bfloat16),
            jax.ShapeDtypeStruct((lists, 2 * length, depth), jnp.bfloat16),
            *[jax.ShapeDtypeStruct(q.shape, q.dtype) for q in queries],
        ),
        in_specs=[ANYWHERE] * (2 + len(queries)),
        out_specs=(WHOLE,) * (2 + len(queries)),
        scratch_shapes=[
            pltpu.VMEM(centroids.shape, jnp.float32),
            pltpu.VMEM(stored.shape, jnp.float32),
            pltpu.SemaphoreType.DMA((lists + 1 + len(queries),)),
        ],
        compiler_params=pltpu.CompilerParams(vmem_limit_bytes=LARGE),
        cost_estimate=pl.CostEstimate(flops=6 * rows * depth, bytes_accessed=8 * rows * depth, transcendentals=0),
        name="prepare",
    )(centroids, stored, *queries)


def score_kernel(blocks_ref, places_ref, counts_ref, *refs, rows_dev):
    *halves, out_ref, queries_ref, parts_ref = refs
    origin = here() >> 1
    chunks = TILE // rows_dev
    first = position(origin)
    for chunk in range(chunks):
        offset = position(chunk if blocks_ref.shape[0] == TILE else pl.program_id(0) * chunks + chunk)
        source = pl.multiple_of((first ^ offset) * rows_dev, rows_dev)
        queries_ref[pl.ds(chunk * rows_dev, rows_dev), :] = blocks_ref[pl.ds(source, rows_dev), :]
    parts_ref[:TILE], parts_ref[TILE:] = split(queries_ref[...])

    def scores(vectors):
        count = vectors.shape[0] // 2
        terms = lax.dot_general(vectors[...], parts_ref[...], NT, preferred_element_type=jnp.float32)
        small = terms[:count, TILE:] + (terms[count:, :TILE] + terms[count:, TILE:])
        return terms[:count, :TILE] + small

    best = [jnp.full((1, TILE), LOWEST, jnp.float32) for _ in range(1 + places_ref.shape[0])]
    for side in range(2):
        centers_ref, vectors_ref = halves[2 * side : 2 * side + 2]
        lists, length = vectors_ref.shape[0], vectors_ref.shape[1] // 2
        place = lax.broadcasted_iota(jnp.int32, (length, TILE), 0)
        best[0] = jnp.maximum(best[0], jnp.max(scores(centers_ref), axis=0, keepdims=True))
        for slot in range(lists):
            usable = jnp.where(place < counts_ref[side, pl.ds(slot, 1), :], scores(vectors_ref.at[slot]), LOWEST)
            found = jnp.max(usable, axis=0, keepdims=True)
            for step in range(places_ref.shape[0]):
                chosen = jnp.where(places_ref[pl.ds(step, 1), :] == slot, found, LOWEST)
                best[1 + step] = jnp.maximum(best[1 + step], chosen)
    best = jnp.concatenate(best, axis=0)
    nothing = jnp.full(best.shape, LOWEST, jnp.float32)
    for chip in range(chunks):
        straight = crossed((pl.program_id(0) * chunks + chip) ^ origin) == (here() & 1)
        out_ref[2 * chip] = jnp.where(straight, best, nothing)
        out_ref[2 * chip + 1] = jnp.where(straight, nothing, best)


def score(rows_dev, blocks, places, counts, *halves):
    half, depth = blocks.shape
    kinds = 1 + places.shape[0]
    rows = halves[0].shape[0] + halves[1].shape[0] * halves[1].shape[1]
    devices = 2 * TILE // rows_dev
    return pl.pallas_call(
        functools.partial(score_kernel, rows_dev=rows_dev),
        out_shape=jax.ShapeDtypeStruct((half // TILE * devices, kinds, TILE), jnp.float32),
        grid=(half // TILE,),
        in_specs=[WHOLE, pl.BlockSpec((kinds - 1, TILE), lambda i: (0, i)), WHOLE, *[WHOLE] * len(halves)],
        out_specs=pl.BlockSpec((devices, kinds, TILE), lambda i: (i, 0, 0)),
        scratch_shapes=[pltpu.VMEM((TILE, depth), jnp.float32), pltpu.VMEM((2 * TILE, depth), jnp.bfloat16)],
        compiler_params=pltpu.CompilerParams(vmem_limit_bytes=LARGE),
        cost_estimate=pl.CostEstimate(flops=8 * rows * half * depth, bytes_accessed=4 * rows * depth, transcendentals=0),
        name="score",
    )(blocks, places, counts, *halves)


def finish_kernel(arrived_ref, coarse_ref, fine_ref, *, rows_dev):
    best = jnp.max(arrived_ref[...], axis=0)
    lane = ((here() >> 1) * rows_dev) % TILE
    best = pltpu.roll(best, (TILE - lane) % TILE, 1)
    coarse_ref[...] = best[0, :rows_dev]
    fine_ref[...] = best[1:, :rows_dev]


def finish(rows_dev, arrived):
    kinds = arrived.shape[1]
    return pl.pallas_call(
        functools.partial(finish_kernel, rows_dev=rows_dev),
        out_shape=(
            jax.ShapeDtypeStruct((rows_dev,), jnp.float32),
            jax.ShapeDtypeStruct((kinds - 1, rows_dev), jnp.float32),
        ),
        in_specs=[WHOLE],
        out_specs=(WHOLE, WHOLE),
        compiler_params=pltpu.CompilerParams(vmem_limit_bytes=SMALL),
        name="finish",
    )(arrived)


def gathered(blocks, stage):
    return [exchanged(blocks, mask | 1) for mask in stage]


def in_hbm(*arrays):
    return [pltpu.with_memory_space_constraint(array, pltpu.HBM) for array in arrays]


def local(queries, centroids, stored, vector_ids, list_home, probes):
    devices = lax.axis_size("group") * lax.axis_size("member")
    rows_dev = queries.shape[0]
    first, *rest = stages()
    arrived = gathered(queries, first)
    theirs = [exchanged(array, 1) for array in (centroids, stored, vector_ids)]
    *own, copied = prepare(*in_hbm(centroids, stored, queries))
    blocks = jnp.concatenate([copied, *arrived], axis=0)
    for number, stage in enumerate(rest):
        blocks, *own = lax.optimization_barrier((blocks, *own))
        arrived = gathered(blocks, stage)
        if number == len(rest) - 1:
            other = prepare(*theirs[:2])
            found = lookup(devices // 2 * rows_dev, *in_hbm(list_home, probes.transpose(1, 0, 2), vector_ids), theirs[2])
            ready = lax.optimization_barrier((*arrived, *found, *own, *other))
            arrived, ready = ready[: len(stage)], ready[len(stage) :]
        blocks = jnp.concatenate([blocks, *arrived], axis=0)
    parts = score(rows_dev, blocks, *ready)
    return finish(rows_dev, lax.all_to_all(parts, BOTH, 0, 0, tiled=True))


def solution(mesh):
    placed = (
        P(BOTH, None),
        P(BOTH, None),
        P("group", "member", None),
        P("group", "member"),
        P(),
        P(),
    )
    return jax.shard_map(
        local,
        mesh=mesh,
        in_specs=placed,
        out_specs=(P(BOTH), P(None, BOTH)),
        check_vma=False,
    )
```

time: 34.4 us -> 32.2 us (0.936)
  local copies, waits for them, and re-layouts: 2.92 us -> 0.01 us
  waiting for transfers between devices: 2.86 us -> 4.71 us
  blocking collectives: 11.8 us -> 10.4 us
  Pallas kernels: 6.04 us -> 7.02 us
  other arithmetic: 0.77 us -> 0.04 us
    unnamed x8 -> x2, local copies, waits for them, and re-layouts: 2.92 us -> 0.01 us
    ppermute x7 -> x9, waiting for transfers between devices: 2.86 us -> 4.71 us  [exchanged(): return lax.ppermute(value, BOTH, [(d, d ^ mask) for d in range(devices)])]
    all_to_all x1, blocking collectives: 11.8 us -> 10.4 us  [local(): return finish(rows_dev, lax.all_to_all(parts, BOTH, 0, 0, tiled=True))]
    pallas_call x4, Pallas kernels: 5.38 us -> 6.36 us  [the longest x2 3.06 us: prepare(): pl.pallas_call(split_kernel, out_shape=(jax.ShapeDtypeStruct((2 * centroi...]
    concatenate x2, other arithmetic: 0.77 us -> 0.04 us  [the longest x1 0.03 us: local(): blocks = jnp.concatenate([blocks, *arrived], axis=0)]
    ppermute x7 -> x9, starting transfers between devices: 8.94 us -> 9.14 us  [exchanged(): return lax.ppermute(value, BOTH, [(d, d ^ mask) for d in range(devices)])]
  transfers between devices with their start and end apart: 7 -> 9, of which waited for: 3 -> 4; matrix products, arithmetic and copies ran while one was open for 0% -> 0% of each run, Pallas kernels for 12% -> 13%
where the time goes in v3:
time: 32.2 us; the launch traced here: 32 us
  blocking collectives  10.4 us (32%)
  starting transfers between devices  9.14 us (28%)
  Pallas kernels  7.02 us (22%)
  waiting for transfers between devices  4.71 us (15%)
  between operations  0.72 us (2%)
    all_to_all x1, blocking collectives, local(): return finish(rows_dev, lax.all_to_all(parts, BOTH, 0, 0, tiled=True))  10.4 us
    ppermute x9, starting transfers between devices, exchanged(): return lax.ppermute(value, BOTH, [(d, d ^ mask) for d in range(devices)])  9.14 us
    ppermute x9, waiting for transfers between devices, exchanged(): return lax.ppermute(value, BOTH, [(d, d ^ mask) for d in range(devices)])  4.71 us
    pallas_call x2, Pallas kernels, prepare(): pl.pallas_call(split_kernel, out_shape=(jax.ShapeDtypeStruct((2 * centroi...  3.06 us
    pallas_call x1, Pallas kernels, score(): pl.pallas_call(functools.partial(score_kernel, rows_dev=rows_dev), out_sh...  2.09 us
    pallas_call x1, Pallas kernels, lookup(): pl.pallas_call(functools.partial(lookup_kernel, lanes=half // blocks), ou...  1.21 us
    pallas_call x1, Pallas kernels, finish(): pl.pallas_call(functools.partial(finish_kernel, rows_dev=rows_dev), out_s...  0.66 us
  transfers between devices with their start and end apart: 9, of which 4 were waited for; matrix products, arithmetic and copies ran while one was open for 0% of the time, Pallas kernels for 13%

profile of v3, /device:TPU:0, one launch (start us, length us, event | category | flops | bytes accessed | tf_op | source)
XLA Modules:
  0.0 32.0 jit_solution(11343794574703721564)
XLA Ops:
  0.6 0.0 copy-start
  0.6 0.5 %collective-permute-start.8 = (f32[4,256,768]{2,1,0:T(8,128)}, f32[4,256,768]{2,1,0:T(8,128)S(1)}, u32[]{:S(2)}, u32[]{:S(2)}) collective-permute-start(f32[4,256,768]{2,1,0:T(8,128)} %stored_hbm.1), channel_id=1, source_target_pairs={{0,1},{1,0},{2,3},{3,2},{4,5},{5,4},{6,7},{7,6},{8,9},{9,8},{10,11... | collective-permute-start | bytes 9437192 | tf_op jit(solution)/shard_map/ppermute | solution.py:34
  1.2 4.7 %collective-permute-start = (f32[8,768]{1,0:T(8,128)}, f32[8,768]{1,0:T(8,128)S(1)}, u32[]{:S(2)}, u32[]{:S(2)}) collective-permute-start(f32[8,768]{1,0:T(8,128)} %refs_0_.1), channel_id=1, source_target_pairs={{0,7},{1,6},{2,5},{3,4},{4,3},{5,2},{6,1},{7,0},{8,15},{9,14},{10,... | collective-permute-start | bytes 73736 | tf_op jit(solution)/shard_map/ppermute | solution.py:34
  5.9 0.0 collective-permute-start.2
  5.9 0.3 %collective-permute-start.1 = (f32[8,768]{1,0:T(8,128)}, f32[8,768]{1,0:T(8,128)S(1)}, u32[]{:S(2)}, u32[]{:S(2)}) collective-permute-start(f32[8,768]{1,0:T(8,128)} %refs_0_.1), channel_id=1, source_target_pairs={{0,5},{1,4},{2,7},{3,6},{4,1},{5,0},{6,3},{7,2},{8,13},{9,12},{10,... | collective-permute-start | bytes 73736 | tf_op jit(solution)/shard_map/ppermute | solution.py:34
  6.2 0.3 %collective-permute-start.7 = (f32[32,768]{1,0:T(8,128)}, f32[32,768]{1,0:T(8,128)S(1)}, u32[]{:S(2)}, u32[]{:S(2)}) collective-permute-start(f32[32,768]{1,0:T(8,128)} %centroids_hbm.1), channel_id=1, source_target_pairs={{0,1},{1,0},{2,3},{3,2},{4,5},{5,4},{6,7},{7,6},{8,9},{9,8},{10,11... | collective-permute-start | bytes 294920 | tf_op jit(solution)/shard_map/ppermute | solution.py:34
  6.6 2.1 %prepare.2 = (bf16[64,768]{1,0:T(8,128)(2,1)S(1)}, bf16[4,512,768]{2,1,0:T(8,128)(2,1)S(1)}, f32[8,768]{1,0:T(8,128)S(1)}) custom-call(f32[32,768]{1,0:T(8,128)} %centroids_hbm.1, f32[4,256,768]{2,1,0:T(8,128)} %stored_hbm.1, f32[8,768]{1,0:T(8,128)} %refs_0_.1), custom_call_target="tpu_custom_call" | custom-call | flops 4866048 | bytes 6488064 | tf_op jit(solution)/shard_map/prepare/pallas_call | solution.py:145
  8.7 0.0 collective-permute-done
  8.7 0.0 copy-done
  8.7 0.2 collective-permute-start.6
  8.9 0.4 %collective-permute-done.2 = f32[8,768]{1,0:T(8,128)S(1)} collective-permute-done((f32[8,768]{1,0:T(8,128)}, f32[8,768]{1,0:T(8,128)S(1)}, u32[]{:S(2)}, u32[]{:S(2)}) %collective-permute-start.2) | collective-permute-done | bytes 24608 | tf_op jit(solution)/shard_map/ppermute | solution.py:34
  9.4 0.9 %collective-permute-done.1 = f32[8,768]{1,0:T(8,128)S(1)} collective-permute-done((f32[8,768]{1,0:T(8,128)}, f32[8,768]{1,0:T(8,128)S(1)}, u32[]{:S(2)}, u32[]{:S(2)}) %collective-permute-start.1) | collective-permute-done | bytes 24608 | tf_op jit(solution)/shard_map/ppermute | solution.py:34
  10.3 1.3 %collective-permute-start.5 = (f32[32,768]{1,0:T(8,128)S(1)}, f32[32,768]{1,0:T(8,128)S(1)}, u32[]{:S(2)}, u32[]{:S(2)}) collective-permute-start(f32[32,768]{1,0:T(8,128)S(1)} %pad_maximum_fusion.1), channel_id=1, source_target_pairs={{0,9},{1,8},{2,11},{3,10},{4,13},{5,12},{6,15},{7,14},{8,1},{9,0},... | collective-permute-start | bytes 294920 | tf_op jit(solution)/shard_map/ppermute | solution.py:34
  11.6 1.6 %collective-permute-start.4 = (f32[32,768]{1,0:T(8,128)S(1)}, f32[32,768]{1,0:T(8,128)S(1)}, u32[]{:S(2)}, u32[]{:S(2)}) collective-permute-start(f32[32,768]{1,0:T(8,128)S(1)} %pad_maximum_fusion.1), channel_id=1, source_target_pairs={{0,17},{1,16},{2,19},{3,18},{4,21},{5,20},{6,23},{7,22},{8,25},{9,... | collective-permute-start | bytes 294920 | tf_op jit(solution)/shard_map/ppermute | solution.py:34
  13.1 0.0 collective-permute-done.6.theirs_hbm
  13.1 0.2 collective-permute-start.3
  13.3 1.2 %lookup.1 = (s32[3,128]{1,0:T(4,128)S(1)}, s32[2,4,128]{2,1,0:T(4,128)S(1)}) custom-call(s32[16]{0:T(128)} %home_hbm.1, s32[3,4,4]{2,1,0:T(4,128)} %bitcast.1, s32[4,256]{1,0:T(4,128)} %ids_hbm.1, s32[4,256]{1,0:T(4,128)S(1)} %collective-permute-done.6.theirs_hbm), custom_call_target="tpu_custom_call" | custom-call | flops 10000 | bytes 100000 | tf_op jit(solution)/shard_map/lookup/pallas_call | solution.py:102
  14.5 0.0 collective-permute-done.7.centroids_hbm
  14.5 0.0 collective-permute-done.8.stored_hbm
  14.5 1.0 %prepare.3 = (bf16[64,768]{1,0:T(8,128)(2,1)S(1)}, bf16[4,512,768]{2,1,0:T(8,128)(2,1)S(1)}) custom-call(f32[32,768]{1,0:T(8,128)S(1)} %collective-permute-done.7.centroids_hbm, f32[4,256,768]{2,1,0:T(8,128)S(1)} %collective-permute-done.8.stored_hbm), custom_call_target="tpu_custom_call" | custom-call | flops 4866048 | bytes 6488064 | tf_op jit(solution)/shard_map/prepare/pallas_call | solution.py:145
  15.5 0.0 collective-permute-done.5
  15.5 2.3 %collective-permute-done.4 = f32[32,768]{1,0:T(8,128)S(1)} collective-permute-done((f32[32,768]{1,0:T(8,128)S(1)}, f32[32,768]{1,0:T(8,128)S(1)}, u32[]{:S(2)}, u32[]{:S(2)}) %collective-permute-start.4) | collective-permute-done | bytes 98336 | tf_op jit(solution)/shard_map/ppermute | solution.py:34
  17.8 1.0 %collective-permute-done.3 = f32[32,768]{1,0:T(8,128)S(1)} collective-permute-done((f32[32,768]{1,0:T(8,128)S(1)}, f32[32,768]{1,0:T(8,128)S(1)}, u32[]{:S(2)}, u32[]{:S(2)}) %collective-permute-start.3) | collective-permute-done | bytes 98336 | tf_op jit(solution)/shard_map/ppermute | solution.py:34
  18.9 2.1 %score.1 = f32[32,4,128]{2,1,0:T(4,128)S(1)} custom-call(f32[128,768]{1,0:T(8,128)S(1)} %pad_maximum_fusion.blocks_ref, s32[3,128]{1,0:T(4,128)S(1)} %get-tuple-element.34.places_ref, s32[2,4,128]{2,1,0:T(4,128)S(1)} %get-tuple-element.35.counts_ref, bf16[64,768]{1,0:T(8,128)(2,1)S(1)} %get-tuple-element.36.refs_0_, ...), custom_call_target="tpu_custom_call" | custom-call | flops 1660944384 | bytes 6488064 | tf_op jit(solution)/shard_map/score/pallas_call | solution.py:207
  21.0 10.4 %all_to_all.5.arrived_ref = f32[32,4,128]{2,1,0:T(4,128)S(1)} all-to-all(f32[32,4,128]{2,1,0:T(4,128)S(1)} %score.1), channel_id=1, replica_groups=mesh['group'=4,'member'=8] {'group','member'}, dimensions={0} | all-to-all | bytes 131072 | tf_op jit(solution)/shard_map/all_to_all | solution.py:269
  31.3 0.7 %finish.1 = (f32[8]{0:T(128)}, f32[3,8]{1,0:T(4,128)}) custom-call(f32[32,4,128]{2,1,0:T(4,128)S(1)} %all_to_all.5.arrived_ref), custom_call_target="tpu_custom_call" | custom-call | tf_op jit(solution)/shard_map/finish/pallas_call | solution.py:230
  (2 shorter events, 0.0 us)
Async XLA Ops:
  0.6 8.1 %copy-start = (s32[4,256]{1,0:T(4,128)S(1)}, s32[4,256]{1,0:T(4,128)}, u32[]{:S(2)}) copy-start(s32[4,256]{1,0:T(4,128)} %ids_hbm.1) | copy-start | bytes 12292
  0.6 13.9 %collective-permute-start.8 = (f32[4,256,768]{2,1,0:T(8,128)}, f32[4,256,768]{2,1,0:T(8,128)S(1)}, u32[]{:S(2)}, u32[]{:S(2)}) collective-permute-start(f32[4,256,768]{2,1,0:T(8,128)} %stored_hbm.1), channel_id=1, source_target_pairs={{0,1},{1,0},{2,3},{3,2},{4,5},{5,4},{6,7},{7,6},{8,9},{9,8},{10,11... | collective-permute-start | bytes 9437192 | tf_op jit(solution)/shard_map/ppermute | solution.py:34
  1.2 7.5 %collective-permute-start = (f32[8,768]{1,0:T(8,128)}, f32[8,768]{1,0:T(8,128)S(1)}, u32[]{:S(2)}, u32[]{:S(2)}) collective-permute-start(f32[8,768]{1,0:T(8,128)} %refs_0_.1), channel_id=1, source_target_pairs={{0,7},{1,6},{2,5},{3,4},{4,3},{5,2},{6,1},{7,0},{8,15},{9,14},{10,... | collective-permute-start | bytes 73736 | tf_op jit(solution)/shard_map/ppermute | solution.py:34
  5.9 3.5 %collective-permute-start.2 = (f32[8,768]{1,0:T(8,128)}, f32[8,768]{1,0:T(8,128)S(1)}, u32[]{:S(2)}, u32[]{:S(2)}) collective-permute-start(f32[8,768]{1,0:T(8,128)} %refs_0_.1), channel_id=1, source_target_pairs={{0,3},{1,2},{2,1},{3,0},{4,7},{5,6},{6,5},{7,4},{8,11},{9,10},{10,... | collective-permute-start | bytes 73736 | tf_op jit(solution)/shard_map/ppermute | solution.py:34
  5.9 4.4 %collective-permute-start.1 = (f32[8,768]{1,0:T(8,128)}, f32[8,768]{1,0:T(8,128)S(1)}, u32[]{:S(2)}, u32[]{:S(2)}) collective-permute-start(f32[8,768]{1,0:T(8,128)} %refs_0_.1), channel_id=1, source_target_pairs={{0,5},{1,4},{2,7},{3,6},{4,1},{5,0},{6,3},{7,2},{8,13},{9,12},{10,... | collective-permute-start | bytes 73736 | tf_op jit(solution)/shard_map/ppermute | solution.py:34
  6.2 8.3 %collective-permute-start.7 = (f32[32,768]{1,0:T(8,128)}, f32[32,768]{1,0:T(8,128)S(1)}, u32[]{:S(2)}, u32[]{:S(2)}) collective-permute-start(f32[32,768]{1,0:T(8,128)} %centroids_hbm.1), channel_id=1, source_target_pairs={{0,1},{1,0},{2,3},{3,2},{4,5},{5,4},{6,7},{7,6},{8,9},{9,8},{10,11... | collective-permute-start | bytes 294920 | tf_op jit(solution)/shard_map/ppermute | solution.py:34
  8.7 4.4 %collective-permute-start.6 = (s32[4,256]{1,0:T(4,128)S(1)}, s32[4,256]{1,0:T(4,128)S(1)}, u32[]{:S(2)}, u32[]{:S(2)}) collective-permute-start(s32[4,256]{1,0:T(4,128)S(1)} %copy-done), channel_id=1, source_target_pairs={{0,1},{1,0},{2,3},{3,2},{4,5},{5,4},{6,7},{7,6},{8,9},{9,8},{10,11... | collective-permute-start | bytes 12296 | tf_op jit(solution)/shard_map/ppermute | solution.py:34
  10.3 5.2 %collective-permute-start.5 = (f32[32,768]{1,0:T(8,128)S(1)}, f32[32,768]{1,0:T(8,128)S(1)}, u32[]{:S(2)}, u32[]{:S(2)}) collective-permute-start(f32[32,768]{1,0:T(8,128)S(1)} %pad_maximum_fusion.1), channel_id=1, source_target_pairs={{0,9},{1,8},{2,11},{3,10},{4,13},{5,12},{6,15},{7,14},{8,1},{9,0},... | collective-permute-start | bytes 294920 | tf_op jit(solution)/shard_map/ppermute | solution.py:34
  11.6 6.3 %collective-permute-start.4 = (f32[32,768]{1,0:T(8,128)S(1)}, f32[32,768]{1,0:T(8,128)S(1)}, u32[]{:S(2)}, u32[]{:S(2)}) collective-permute-start(f32[32,768]{1,0:T(8,128)S(1)} %pad_maximum_fusion.1), channel_id=1, source_target_pairs={{0,17},{1,16},{2,19},{3,18},{4,21},{5,20},{6,23},{7,22},{8,25},{9,... | collective-permute-start | bytes 294920 | tf_op jit(solution)/shard_map/ppermute | solution.py:34
  13.1 5.7 %collective-permute-start.3 = (f32[32,768]{1,0:T(8,128)S(1)}, f32[32,768]{1,0:T(8,128)S(1)}, u32[]{:S(2)}, u32[]{:S(2)}) collective-permute-start(f32[32,768]{1,0:T(8,128)S(1)} %pad_maximum_fusion.1), channel_id=1, source_target_pairs={{0,25},{1,24},{2,27},{3,26},{4,29},{5,28},{6,31},{7,30},{8,17},{9,... | collective-permute-start | bytes 294920 | tf_op jit(solution)/shard_map/ppermute | solution.py:34

commit v4 on v3

v4 whole, which is shorter than its diff:
```python
import functools

import jax
import jax.numpy as jnp
from jax import lax
from jax.experimental import pallas as pl
from jax.experimental.pallas import tpu as pltpu
from jax.sharding import PartitionSpec as P

LOWEST = -1e30
TILE = 128
EIGHT = jnp.float8_e4m3fn
SCALE = 2.0**16
BOTH = ("group", "member")
NT = (((1,), (1,)), ((), ()))
LARGE = 20 * 2**20
SMALL = 10 * 2**20
WHOLE = pl.BlockSpec(memory_space=pltpu.VMEM)
ANYWHERE = pl.BlockSpec(memory_space=pl.ANY)


def stages():
    members, groups = lax.axis_size("member"), lax.axis_size("group")
    inner = [1 << k for k in range(1, members.bit_length() - 1)]
    outer = [members << k for k in range(groups.bit_length() - 1)]
    listed = []
    for bits, order in ((inner, (2, 1, 3)), (outer, (3, 2, 1))):
        for at in range(0, len(bits), 2):
            pair = bits[at : at + 2]
            listed.append([pair[0] * value | 1 for value in order[: 2 * len(pair) - 1] if len(pair) == 2] or [pair[0] | 1])
    return listed


def exchanged(value, mask):
    devices = lax.axis_size("group") * lax.axis_size("member")
    return lax.ppermute(value, BOTH, [(d, d ^ mask) for d in range(devices)])


def positions():
    offsets = [0]
    for stage in stages():
        offsets = [offset ^ (mask >> 1) for mask in [0, *stage] for offset in offsets]
    return [offsets.index(1 << k) for k in range(len(offsets).bit_length() - 1)]


def position(chip):
    place = 0
    for k, at in enumerate(positions()):
        place = place ^ (((chip >> k) & 1) * at)
    return place


def here():
    return lax.axis_index("group") * lax.axis_size("member") + lax.axis_index("member")


def crossed(chips):
    found = 0
    for stage in stages():
        bits = functools.reduce(lambda a, b: a | b, stage) >> 1
        for mask in stage:
            if mask & 1:
                found = found ^ jnp.where((chips & bits) == mask >> 1, 1, 0)
    return found


def split(value):
    high = value.astype(jnp.bfloat16)
    return high, value - high.astype(jnp.float32)


def copy_all(pairs, sems):
    copies = [pltpu.make_async_copy(source, target, sems.at[k]) for k, (source, target) in enumerate(pairs)]
    for copy in copies:
        copy.start()
    return copies


def lookup_kernel(home_hbm, probes_hbm, queries_hbm, places_ref, queries_ref, home_ref, probes_ref, sems, *, lists, lanes):
    copies = copy_all([(home_hbm, home_ref), (probes_hbm, probes_ref), (queries_hbm, queries_ref)], sems)
    copies[0].wait()
    copies[1].wait()
    group = lax.axis_index("group")
    steps, blocks, probed = probes_ref.shape
    lane_block = lax.broadcasted_iota(jnp.int32, (1, places_ref.shape[1]), 1) // lanes
    for step in range(steps):

        def of_block(b, row, step=step):
            place = jnp.int32(-1)
            for j in range(probed):
                slot = home_ref[probes_ref[step, b, j]]
                place = jnp.where(slot // lists == group, slot % lists, place)
            return jnp.where(lane_block == b, place, row)

        row = jnp.full(lane_block.shape, -1, jnp.int32)
        places_ref[pl.ds(step, 1), :] = lax.fori_loop(0, blocks, of_block, row)
    copies[2].wait()


def lookup(half, lists, list_home, probes, queries):
    steps, blocks, _ = probes.shape
    return pl.pallas_call(
        functools.partial(lookup_kernel, lists=lists, lanes=half // blocks),
        out_shape=(
            jax.ShapeDtypeStruct((steps, half), jnp.int32),
            jax.ShapeDtypeStruct(queries.shape, queries.dtype),
        ),
        in_specs=[ANYWHERE] * 3,
        out_specs=(WHOLE, WHOLE),
        scratch_shapes=[
            pltpu.SMEM(list_home.shape, jnp.int32),
            pltpu.SMEM(probes.shape, jnp.int32),
            pltpu.SemaphoreType.DMA((3,)),
        ],
        compiler_params=pltpu.CompilerParams(vmem_limit_bytes=SMALL),
        cost_estimate=pl.CostEstimate(flops=10000, bytes_accessed=100000, transcendentals=0),
        name="lookup",
    )(list_home, probes, queries)


def split_vectors(value):
    high, low = split(value)
    return high, (low * SCALE).astype(EIGHT)


def split_lists(centroids_ref, ids_ref, stored_ref, *refs, arrived=lambda k: None):
    centers_ref, centers_low_ref, counts_ref, vectors_ref, vectors_low_ref = refs
    arrived(0)
    arrived(1)
    centers_ref[...], centers_low_ref[...] = split_vectors(centroids_ref[...])
    valid = jnp.sum((ids_ref[...] >= 0).astype(jnp.float32), axis=1, keepdims=True)
    counts_ref[...] = jnp.broadcast_to(valid, counts_ref.shape).astype(jnp.int32)
    for k in range(stored_ref.shape[0]):
        arrived(2 + k)
        vectors_ref[k], vectors_low_ref[k] = split_vectors(stored_ref[k])


def copied_kernel(centroids_hbm, ids_hbm, stored_hbm, *refs):
    *outs, centroids_ref, ids_ref, stored_ref, sems = refs
    lists = stored_ref.shape[0]
    pairs = [(centroids_hbm, centroids_ref), (ids_hbm, ids_ref), *[(stored_hbm.at[k], stored_ref.at[k]) for k in range(lists)]]
    copies = copy_all(pairs, sems)
    split_lists(centroids_ref, ids_ref, stored_ref, *outs, arrived=lambda k: copies[k].wait())


def prepare(centroids, ids, stored, copied):
    lists, length, depth = stored.shape
    rows = lists * length + centroids.shape[0]
    scratch = [pltpu.VMEM(array.shape, array.dtype) for array in (centroids, ids, stored)]
    return pl.pallas_call(
        copied_kernel if copied else split_lists,
        out_shape=(
            jax.ShapeDtypeStruct(centroids.shape, jnp.bfloat16),
            jax.ShapeDtypeStruct(centroids.shape, EIGHT),
            jax.ShapeDtypeStruct((lists, TILE), jnp.int32),
            jax.ShapeDtypeStruct(stored.shape, jnp.bfloat16),
            jax.ShapeDtypeStruct(stored.shape, EIGHT),
        ),
        in_specs=[ANYWHERE if copied else WHOLE] * 3,
        out_specs=(WHOLE,) * 5,
        scratch_shapes=[*scratch, pltpu.SemaphoreType.DMA((2 + lists,))] if copied else [],
        compiler_params=pltpu.CompilerParams(vmem_limit_bytes=SMALL),
        cost_estimate=pl.CostEstimate(flops=6 * rows * depth, bytes_accessed=8 * rows * depth, transcendentals=0),
        name="prepare",
    )(centroids, ids, stored)


def score_kernel(blocks_ref, places_ref, *refs, rows_dev):
    *halves, out_ref, queries_ref, parts_ref, eighth_ref = refs
    origin = here() >> 1
    chunks = TILE // rows_dev
    first = position(origin)
    for chunk in range(chunks):
        offset = position(chunk if blocks_ref.shape[0] == TILE else pl.program_id(0) * chunks + chunk)
        source = pl.multiple_of((first ^ offset) * rows_dev, rows_dev)
        queries_ref[pl.ds(chunk * rows_dev, rows_dev), :] = blocks_ref[pl.ds(source, rows_dev), :]
    high, low = split(queries_ref[...])
    parts_ref[:TILE], parts_ref[TILE:] = high, low.astype(jnp.bfloat16)
    eighth_ref[...] = queries_ref[...].astype(EIGHT)

    def scores(vectors, vectors_low):
        terms = lax.dot_general(vectors[...], parts_ref[...], NT, preferred_element_type=jnp.float32)
        rest = lax.dot_general(vectors_low[...], eighth_ref[...], NT, preferred_element_type=jnp.float32)
        return terms[:, :TILE] + (terms[:, TILE:] + rest * (1 / SCALE))

    best = [jnp.full((1, TILE), LOWEST, jnp.float32) for _ in range(1 + places_ref.shape[0])]
    for side in range(2):
        centers_ref, centers_low_ref, counts_ref, vectors_ref, vectors_low_ref = halves[5 * side : 5 * side + 5]
        lists, length = vectors_ref.shape[:2]
        place = lax.broadcasted_iota(jnp.int32, (length, TILE), 0)
        best[0] = jnp.maximum(best[0], jnp.max(scores(centers_ref, centers_low_ref), axis=0, keepdims=True))
        for slot in range(lists):
            usable = jnp.where(place < counts_ref[pl.ds(slot, 1), :], scores(vectors_ref.at[slot], vectors_low_ref.at[slot]), LOWEST)
            found = jnp.max(usable, axis=0, keepdims=True)
            for step in range(places_ref.shape[0]):
                chosen = jnp.where(places_ref[pl.ds(step, 1), :] == slot, found, LOWEST)
                best[1 + step] = jnp.maximum(best[1 + step], chosen)
    best = [pltpu.roll(row, kind * rows_dev, 1) if kind else row for kind, row in enumerate(best)]
    lane_chip = lax.broadcasted_iota(jnp.int32, (1, TILE), 1) // rows_dev
    nothing = jnp.full((1, TILE), LOWEST, jnp.float32)
    for chip in range(chunks):
        row = best[0]
        for kind in range(1, len(best)):
            row = jnp.where(lane_chip == (chip + kind) % chunks, best[kind], row)
        straight = crossed((pl.program_id(0) * chunks + chip) ^ origin) == (here() & 1)
        out_ref[2 * chip] = jnp.where(straight, row, nothing)
        out_ref[2 * chip + 1] = jnp.where(straight, nothing, row)


def score(rows_dev, blocks, places, *halves):
    half, depth = blocks.shape
    kinds = 1 + places.shape[0]
    rows = 2 * (halves[0].shape[0] + halves[3].shape[0] * halves[3].shape[1])
    devices = 2 * TILE // rows_dev
    return pl.pallas_call(
        functools.partial(score_kernel, rows_dev=rows_dev),
        out_shape=jax.ShapeDtypeStruct((half // TILE * devices, 1, TILE), jnp.float32),
        grid=(half // TILE,),
        in_specs=[WHOLE, pl.BlockSpec((kinds - 1, TILE), lambda i: (0, i)), *[WHOLE] * len(halves)],
        out_specs=pl.BlockSpec((devices, 1, TILE), lambda i: (i, 0, 0)),
        scratch_shapes=[
            pltpu.VMEM((TILE, depth), jnp.float32),
            pltpu.VMEM((2 * TILE, depth), jnp.bfloat16),
            pltpu.VMEM((TILE, depth), EIGHT),
        ],
        compiler_params=pltpu.CompilerParams(vmem_limit_bytes=LARGE),
        cost_estimate=pl.CostEstimate(flops=8 * rows * half * depth, bytes_accessed=4 * rows * depth, transcendentals=0),
        name="score",
    )(blocks, places, *halves)


def finish_kernel(arrived_ref, coarse_ref, fine_ref, *, rows_dev):
    best = jnp.max(arrived_ref[...], axis=0)
    lane = ((here() >> 1) * rows_dev) % TILE
    best = pltpu.roll(best, (TILE - lane) % TILE, 1)
    coarse_ref[...] = best[0, :rows_dev]
    for step in range(fine_ref.shape[0]):
        fine_ref[pl.ds(step, 1), :] = best[:, (1 + step) * rows_dev : (2 + step) * rows_dev]


def finish(rows_dev, steps, arrived):
    return pl.pallas_call(
        functools.partial(finish_kernel, rows_dev=rows_dev),
        out_shape=(
            jax.ShapeDtypeStruct((rows_dev,), jnp.float32),
            jax.ShapeDtypeStruct((steps, rows_dev), jnp.float32),
        ),
        in_specs=[WHOLE],
        out_specs=(WHOLE, WHOLE),
        compiler_params=pltpu.CompilerParams(vmem_limit_bytes=SMALL),
        name="finish",
    )(arrived)


def gathered(blocks, stage):
    return [exchanged(blocks, mask) for mask in stage]


def in_hbm(*arrays):
    return [pltpu.with_memory_space_constraint(array, pltpu.HBM) for array in arrays]


def local(queries, centroids, stored, vector_ids, list_home, probes):
    devices = lax.axis_size("group") * lax.axis_size("member")
    rows_dev, lists = queries.shape[0], stored.shape[0]
    first, *rest = stages()
    arrived = gathered(queries, first)
    mine = (centroids, vector_ids, stored)
    theirs = [exchanged(array, 1) for array in mine]
    places, copied = lookup(devices // 2 * rows_dev, lists, *in_hbm(list_home, probes.transpose(1, 0, 2), queries))
    blocks = jnp.concatenate([copied, *arrived], axis=0)
    for number, stage in enumerate(rest):
        if number == len(rest) - 1:
            blocks, places, *mine = lax.optimization_barrier((blocks, places, *mine))
        arrived = gathered(blocks, stage)
        if number == len(rest) - 1:
            ready = prepare(*in_hbm(*mine), True), prepare(*theirs, False)
            arrived, ready = lax.optimization_barrier((arrived, ready))
        blocks = jnp.concatenate([blocks, *arrived], axis=0)
    parts = score(rows_dev, blocks, places, *ready[0], *ready[1])
    return finish(rows_dev, probes.shape[1], lax.all_to_all(parts, BOTH, 0, 0, tiled=True))


def solution(mesh):
    placed = (
        P(BOTH, None),
        P(BOTH, None),
        P("group", "member", None),
        P("group", "member"),
        P(),
        P(),
    )
    return jax.shard_map(
        local,
        mesh=mesh,
        in_specs=placed,
        out_specs=(P(BOTH), P(None, BOTH)),
        check_vma=False,
    )
```

time: 32.2 us -> 31.4 us (0.975)
  blocking collectives: 10.4 us -> 9.74 us
    all_to_all x1, blocking collectives: 10.4 us -> 9.74 us  [local(): lax.all_to_all(parts, BOTH, 0, 0, tiled=True)]
  transfers between devices with their start and end apart: 9 -> 9, of which waited for: 4 -> 3; matrix products, arithmetic and copies ran while one was open for 0% -> 0% of each run, Pallas kernels for 13% -> 13%
where the time goes in v4:
time: 31.4 us; the launch traced here: 31.2 us
  blocking collectives  9.74 us (31%)
  starting transfers between devices  9.09 us (29%)
  Pallas kernels  6.86 us (22%)
  waiting for transfers between devices  4.76 us (15%)
  between operations  0.71 us (2%)
    all_to_all x1, blocking collectives, local(): lax.all_to_all(parts, BOTH, 0, 0, tiled=True)  9.74 us
    ppermute x9, starting transfers between devices, exchanged(): return lax.ppermute(value, BOTH, [(d, d ^ mask) for d in range(devices)])  9.09 us
    ppermute x9, waiting for transfers between devices, exchanged(): return lax.ppermute(value, BOTH, [(d, d ^ mask) for d in range(devices)])  4.76 us
    pallas_call x2, Pallas kernels, prepare(): pl.pallas_call(copied_kernel if copied else split_lists, out_shape=(jax.S...  2.97 us
    pallas_call x1, Pallas kernels, score(): pl.pallas_call(functools.partial(score_kernel, rows_dev=rows_dev), out_sh...  1.96 us
    pallas_call x1, Pallas kernels, lookup(): pl.pallas_call(functools.partial(lookup_kernel, lists=lists, lanes=half /...  1.2 us
    pallas_call x1, Pallas kernels, finish(): pl.pallas_call(functools.partial(finish_kernel, rows_dev=rows_dev), out_s...  0.73 us
  transfers between devices with their start and end apart: 9, of which 3 were waited for; matrix products, arithmetic and copies ran while one was open for 0% of the time, Pallas kernels for 13%

profile of v4, /device:TPU:0, one launch (start us, length us, event | category | flops | bytes accessed | tf_op | source)
XLA Modules:
  0.0 31.2 jit_solution(10426701896974498117)
XLA Ops:
  0.6 0.5 %collective-permute-start.8 = (f32[4,256,768]{2,1,0:T(8,128)}, f32[4,256,768]{2,1,0:T(8,128)S(1)}, u32[]{:S(2)}, u32[]{:S(2)}) collective-permute-start(f32[4,256,768]{2,1,0:T(8,128)} %stored_hbm), channel_id=1, source_target_pairs={{0,1},{1,0},{2,3},{3,2},{4,5},{5,4},{6,7},{7,6},{8,9},{9,8},{10,11... | collective-permute-start | bytes 9437192 | tf_op jit(solution)/shard_map/ppermute | solution.py:36
  1.1 3.7 %collective-permute-start = (f32[8,768]{1,0:T(8,128)}, f32[8,768]{1,0:T(8,128)S(1)}, u32[]{:S(2)}, u32[]{:S(2)}) collective-permute-start(f32[8,768]{1,0:T(8,128)} %queries_hbm.1), channel_id=1, source_target_pairs={{0,5},{1,4},{2,7},{3,6},{4,1},{5,0},{6,3},{7,2},{8,13},{9,12},{10,... | collective-permute-start | bytes 73736 | tf_op jit(solution)/shard_map/ppermute | solution.py:36
  4.9 1.0 %collective-permute-start.2 = (f32[8,768]{1,0:T(8,128)}, f32[8,768]{1,0:T(8,128)S(1)}, u32[]{:S(2)}, u32[]{:S(2)}) collective-permute-start(f32[8,768]{1,0:T(8,128)} %queries_hbm.1), channel_id=1, source_target_pairs={{0,7},{1,6},{2,5},{3,4},{4,3},{5,2},{6,1},{7,0},{8,15},{9,14},{10,... | collective-permute-start | bytes 73736 | tf_op jit(solution)/shard_map/ppermute | solution.py:36
  5.9 0.2 collective-permute-start.1
  6.1 0.4 %collective-permute-start.7 = (s32[4,256]{1,0:T(4,128)}, s32[4,256]{1,0:T(4,128)S(1)}, u32[]{:S(2)}, u32[]{:S(2)}) collective-permute-start(s32[4,256]{1,0:T(4,128)} %ids_hbm), channel_id=1, source_target_pairs={{0,1},{1,0},{2,3},{3,2},{4,5},{5,4},{6,7},{7,6},{8,9},{9,8},{10,11... | collective-permute-start | bytes 12296 | tf_op jit(solution)/shard_map/ppermute | solution.py:36
  6.6 1.2 %lookup.1 = (s32[3,128]{1,0:T(4,128)S(1)}, f32[8,768]{1,0:T(8,128)S(1)}) custom-call(s32[16]{0:T(128)} %home_hbm.1, s32[3,4,4]{2,1,0:T(4,128)} %bitcast.1, f32[8,768]{1,0:T(8,128)} %queries_hbm.1), custom_call_target="tpu_custom_call" | custom-call | flops 10000 | bytes 100000 | tf_op jit(solution)/shard_map/lookup/pallas_call | solution.py:102
  7.8 0.0 collective-permute-done
  7.8 0.1 collective-permute-start.6
  7.9 2.3 %collective-permute-done.2 = f32[8,768]{1,0:T(8,128)S(1)} collective-permute-done((f32[8,768]{1,0:T(8,128)}, f32[8,768]{1,0:T(8,128)S(1)}, u32[]{:S(2)}, u32[]{:S(2)}) %collective-permute-start.2) | collective-permute-done | bytes 24608 | tf_op jit(solution)/shard_map/ppermute | solution.py:36
  10.2 0.0 collective-permute-done.1
  10.3 1.3 %collective-permute-start.5 = (f32[32,768]{1,0:T(8,128)S(1)}, f32[32,768]{1,0:T(8,128)S(1)}, u32[]{:S(2)}, u32[]{:S(2)}) collective-permute-start(f32[32,768]{1,0:T(8,128)S(1)} %pad_maximum_fusion.1), channel_id=1, source_target_pairs={{0,9},{1,8},{2,11},{3,10},{4,13},{5,12},{6,15},{7,14},{8,1},{9,0},... | collective-permute-start | bytes 294920 | tf_op jit(solution)/shard_map/ppermute | solution.py:36
  11.6 1.5 %collective-permute-start.4 = (f32[32,768]{1,0:T(8,128)S(1)}, f32[32,768]{1,0:T(8,128)S(1)}, u32[]{:S(2)}, u32[]{:S(2)}) collective-permute-start(f32[32,768]{1,0:T(8,128)S(1)} %pad_maximum_fusion.1), channel_id=1, source_target_pairs={{0,17},{1,16},{2,19},{3,18},{4,21},{5,20},{6,23},{7,22},{8,25},{9,... | collective-permute-start | bytes 294920 | tf_op jit(solution)/shard_map/ppermute | solution.py:36
  13.1 0.0 collective-permute-done.7.ids_ref
  13.1 0.2 collective-permute-start.3
  13.3 2.1 %prepare.2 = (bf16[32,768]{1,0:T(8,128)(2,1)S(1)}, f8e4m3fn[32,768]{1,0:T(32,128)(4,1)S(1)}, s32[4,128]{1,0:T(4,128)S(1)}, bf16[4,256,768]{2,1,0:T(8,128)(2,1)S(1)}, f8e4m3fn[4,256,768]{2,1,0:T(32,128)(4,1)S(1)}) custom-call(f32[32,768]{1,0:T(8,128)} %centroids_hbm, s32[4,256]{1,0:T(4,128)} %ids_hbm, f32[4,256,768]{2,1,0:T(8,128)} %stored_hbm), custom_call_target="tpu_custom_call" | custom-call | flops 4866048 | bytes 6488064 | tf_op jit(solution)/shard_map/prepare/pallas_call | solution.py:150
  15.4 0.0 collective-permute-done.6.centroids_ref
  15.4 0.0 collective-permute-done.8.stored_ref
  15.4 0.9 %prepare.3 = (bf16[32,768]{1,0:T(8,128)(2,1)S(1)}, f8e4m3fn[32,768]{1,0:T(32,128)(4,1)S(1)}, s32[4,128]{1,0:T(4,128)S(1)}, bf16[4,256,768]{2,1,0:T(8,128)(2,1)S(1)}, f8e4m3fn[4,256,768]{2,1,0:T(32,128)(4,1)S(1)}) custom-call(f32[32,768]{1,0:T(8,128)S(1)} %collective-permute-done.6.centroids_ref, s32[4,256]{1,0:T(4,128)S(1)} %collective-permute-done.7.ids_ref, ...), custom_call_target="tpu_custom_call" | custom-call | flops 4866048 | bytes 6488064 | tf_op jit(solution)/shard_map/prepare/pallas_call | solution.py:150
  16.3 0.0 collective-permute-done.5
  16.3 1.5 %collective-permute-done.4 = f32[32,768]{1,0:T(8,128)S(1)} collective-permute-done((f32[32,768]{1,0:T(8,128)S(1)}, f32[32,768]{1,0:T(8,128)S(1)}, u32[]{:S(2)}, u32[]{:S(2)}) %collective-permute-start.4) | collective-permute-done | bytes 98336 | tf_op jit(solution)/shard_map/ppermute | solution.py:36
  17.8 0.9 %collective-permute-done.3 = f32[32,768]{1,0:T(8,128)S(1)} collective-permute-done((f32[32,768]{1,0:T(8,128)S(1)}, f32[32,768]{1,0:T(8,128)S(1)}, u32[]{:S(2)}, u32[]{:S(2)}) %collective-permute-start.3) | collective-permute-done | bytes 98336 | tf_op jit(solution)/shard_map/ppermute | solution.py:36
  18.7 2.0 %score.1 = f32[32,1,128]{2,1,0:T(1,128)S(1)} custom-call(f32[128,768]{1,0:T(8,128)S(1)} %pad_maximum_fusion.blocks_ref, s32[3,128]{1,0:T(4,128)S(1)} %get-tuple-element.51.places_ref, bf16[32,768]{1,0:T(8,128)(2,1)S(1)} %get-tuple-element.52.refs_0_, f8e4m3fn[32,768]{1,0:T(32,128)(4,1)S(1)} %get-tuple-element.53.refs_1_, ...), custom_call_target="tpu_custom_call" | custom-call | flops 1660944384 | bytes 6488064 | tf_op jit(solution)/shard_map/score/pallas_call | solution.py:215
  20.7 9.7 %all_to_all.5.arrived_ref = f32[32,1,128]{2,1,0:T(1,128)S(1)} all-to-all(f32[32,1,128]{2,1,0:T(1,128)S(1)} %score.1), channel_id=1, replica_groups=mesh['group'=4,'member'=8] {'group','member'}, dimensions={0} | all-to-all | bytes 32768 | tf_op jit(solution)/shard_map/all_to_all | solution.py:281
  30.5 0.7 %finish.1 = (f32[8]{0:T(128)}, f32[3,8]{1,0:T(4,128)}) custom-call(f32[32,1,128]{2,1,0:T(1,128)S(1)} %all_to_all.5.arrived_ref), custom_call_target="tpu_custom_call" | custom-call | tf_op jit(solution)/shard_map/finish/pallas_call | solution.py:242
  (2 shorter events, 0.0 us)
Async XLA Ops:
  0.6 14.8 %collective-permute-start.8 = (f32[4,256,768]{2,1,0:T(8,128)}, f32[4,256,768]{2,1,0:T(8,128)S(1)}, u32[]{:S(2)}, u32[]{:S(2)}) collective-permute-start(f32[4,256,768]{2,1,0:T(8,128)} %stored_hbm), channel_id=1, source_target_pairs={{0,1},{1,0},{2,3},{3,2},{4,5},{5,4},{6,7},{7,6},{8,9},{9,8},{10,11... | collective-permute-start | bytes 9437192 | tf_op jit(solution)/shard_map/ppermute | solution.py:36
  1.1 6.6 %collective-permute-start = (f32[8,768]{1,0:T(8,128)}, f32[8,768]{1,0:T(8,128)S(1)}, u32[]{:S(2)}, u32[]{:S(2)}) collective-permute-start(f32[8,768]{1,0:T(8,128)} %queries_hbm.1), channel_id=1, source_target_pairs={{0,5},{1,4},{2,7},{3,6},{4,1},{5,0},{6,3},{7,2},{8,13},{9,12},{10,... | collective-permute-start | bytes 73736 | tf_op jit(solution)/shard_map/ppermute | solution.py:36
  4.9 5.4 %collective-permute-start.2 = (f32[8,768]{1,0:T(8,128)}, f32[8,768]{1,0:T(8,128)S(1)}, u32[]{:S(2)}, u32[]{:S(2)}) collective-permute-start(f32[8,768]{1,0:T(8,128)} %queries_hbm.1), channel_id=1, source_target_pairs={{0,7},{1,6},{2,5},{3,4},{4,3},{5,2},{6,1},{7,0},{8,15},{9,14},{10,... | collective-permute-start | bytes 73736 | tf_op jit(solution)/shard_map/ppermute | solution.py:36
  5.9 4.4 %collective-permute-start.1 = (f32[8,768]{1,0:T(8,128)}, f32[8,768]{1,0:T(8,128)S(1)}, u32[]{:S(2)}, u32[]{:S(2)}) collective-permute-start(f32[8,768]{1,0:T(8,128)} %queries_hbm.1), channel_id=1, source_target_pairs={{0,3},{1,2},{2,1},{3,0},{4,7},{5,6},{6,5},{7,4},{8,11},{9,10},{10,... | collective-permute-start | bytes 73736 | tf_op jit(solution)/shard_map/ppermute | solution.py:36
  6.1 6.9 %collective-permute-start.7 = (s32[4,256]{1,0:T(4,128)}, s32[4,256]{1,0:T(4,128)S(1)}, u32[]{:S(2)}, u32[]{:S(2)}) collective-permute-start(s32[4,256]{1,0:T(4,128)} %ids_hbm), channel_id=1, source_target_pairs={{0,1},{1,0},{2,3},{3,2},{4,5},{5,4},{6,7},{7,6},{8,9},{9,8},{10,11... | collective-permute-start | bytes 12296 | tf_op jit(solution)/shard_map/ppermute | solution.py:36
  7.8 7.6 %collective-permute-start.6 = (f32[32,768]{1,0:T(8,128)}, f32[32,768]{1,0:T(8,128)S(1)}, u32[]{:S(2)}, u32[]{:S(2)}) collective-permute-start(f32[32,768]{1,0:T(8,128)} %centroids_hbm), channel_id=1, source_target_pairs={{0,1},{1,0},{2,3},{3,2},{4,5},{5,4},{6,7},{7,6},{8,9},{9,8},{10,11... | collective-permute-start | bytes 294920 | tf_op jit(solution)/shard_map/ppermute | solution.py:36
  10.3 6.0 %collective-permute-start.5 = (f32[32,768]{1,0:T(8,128)S(1)}, f32[32,768]{1,0:T(8,128)S(1)}, u32[]{:S(2)}, u32[]{:S(2)}) collective-permute-start(f32[32,768]{1,0:T(8,128)S(1)} %pad_maximum_fusion.1), channel_id=1, source_target_pairs={{0,9},{1,8},{2,11},{3,10},{4,13},{5,12},{6,15},{7,14},{8,1},{9,0},... | collective-permute-start | bytes 294920 | tf_op jit(solution)/shard_map/ppermute | solution.py:36
  11.6 6.3 %collective-permute-start.4 = (f32[32,768]{1,0:T(8,128)S(1)}, f32[32,768]{1,0:T(8,128)S(1)}, u32[]{:S(2)}, u32[]{:S(2)}) collective-permute-start(f32[32,768]{1,0:T(8,128)S(1)} %pad_maximum_fusion.1), channel_id=1, source_target_pairs={{0,17},{1,16},{2,19},{3,18},{4,21},{5,20},{6,23},{7,22},{8,25},{9,... | collective-permute-start | bytes 294920 | tf_op jit(solution)/shard_map/ppermute | solution.py:36
  13.1 5.7 %collective-permute-start.3 = (f32[32,768]{1,0:T(8,128)S(1)}, f32[32,768]{1,0:T(8,128)S(1)}, u32[]{:S(2)}, u32[]{:S(2)}) collective-permute-start(f32[32,768]{1,0:T(8,128)S(1)} %pad_maximum_fusion.1), channel_id=1, source_target_pairs={{0,25},{1,24},{2,27},{3,26},{4,29},{5,28},{6,31},{7,30},{8,17},{9,... | collective-permute-start | bytes 294920 | tf_op jit(solution)/shard_map/ppermute | solution.py:36

commit v5 on v4

--- a/solution.py
+++ b/solution.py
@@ -19,34 +19,38 @@
 ANYWHERE = pl.BlockSpec(memory_space=pl.ANY)
 
 
+def parity(index):
+    return bin(index).count("1") % 2
+
+
 def stages():
     members, groups = lax.axis_size("member"), lax.axis_size("group")
     inner = [1 << k for k in range(1, members.bit_length() - 1)]
     outer = [members << k for k in range(groups.bit_length() - 1)]
-    listed = []
-    for bits, order in ((inner, (2, 1, 3)), (outer, (3, 2, 1))):
-        for at in range(0, len(bits), 2):
-            pair = bits[at : at + 2]
-            listed.append([pair[0] * value | 1 for value in order[: 2 * len(pair) - 1] if len(pair) == 2] or [pair[0] | 1])
-    return listed
-
-
-def exchanged(value, mask):
+    pairs = [bits[at : at + 2] for bits in (inner, outer) for at in range(0, len(bits), 2)]
+    mirrored = pairs[::-1] if [len(p) for p in pairs] == [len(p) for p in pairs[::-1]] else pairs
+
+    def masks(pair, last):
+        order = (2, 1, 3) if pair[0] < members else (1, 3, 2) if last else (3, 1, 2)
+        chosen = [pair[0] * value for value in order] if len(pair) == 2 else pair
+        return [mask | parity(mask) for mask in chosen]
+
+    count = len(pairs)
+    return [list(zip(masks(pairs[k], k == count - 1), masks(mirrored[k], k == count - 1))) for k in range(count)]
+
+
+def exchanged(value, masks):
     devices = lax.axis_size("group") * lax.axis_size("member")
-    return lax.ppermute(value, BOTH, [(d, d ^ mask) for d in range(devices)])
-
-
-def positions():
+    return lax.ppermute(value, BOTH, [(d, d ^ masks[parity(d)]) for d in range(devices)])
+
+
+def position(chip, odd):
     offsets = [0]
     for stage in stages():
-        offsets = [offset ^ (mask >> 1) for mask in [0, *stage] for offset in offsets]
-    return [offsets.index(1 << k) for k in range(len(offsets).bit_length() - 1)]
-
-
-def position(chip):
+        offsets = [offset ^ (mask >> 1) for mask in [0, *[masks[odd] for masks in stage]] for offset in offsets]
     place = 0
-    for k, at in enumerate(positions()):
-        place = place ^ (((chip >> k) & 1) * at)
+    for k in range(len(offsets).bit_length() - 1):
+        place = place ^ (((chip >> k) & 1) * offsets.index(1 << k))
     return place
 
 
@@ -54,13 +58,10 @@
     return lax.axis_index("group") * lax.axis_size("member") + lax.axis_index("member")
 
 
-def crossed(chips):
+def parity_of(index, count):
     found = 0
-    for stage in stages():
-        bits = functools.reduce(lambda a, b: a | b, stage) >> 1
-        for mask in stage:
-            if mask & 1:
-                found = found ^ jnp.where((chips & bits) == mask >> 1, 1, 0)
+    for k in range(count.bit_length() - 1):
+        found = found ^ ((index >> k) & 1)
     return found
 
 
@@ -167,11 +168,16 @@
 
 def score_kernel(blocks_ref, places_ref, *refs, rows_dev):
     *halves, out_ref, queries_ref, parts_ref, eighth_ref = refs
-    origin = here() >> 1
+    devices = lax.axis_size("group") * lax.axis_size("member")
+    odd = parity_of(here(), devices)
     chunks = TILE // rows_dev
-    first = position(origin)
+
+    def place_of(chip):
+        return jnp.where(odd == 1, position(chip, 1), position(chip, 0))
+
+    first = place_of(here() >> 1)
     for chunk in range(chunks):
-        offset = position(chunk if blocks_ref.shape[0] == TILE else pl.program_id(0) * chunks + chunk)
+        offset = place_of(chunk if blocks_ref.shape[0] == TILE else pl.program_id(0) * chunks + chunk)
         source = pl.multiple_of((first ^ offset) * rows_dev, rows_dev)
         queries_ref[pl.ds(chunk * rows_dev, rows_dev), :] = blocks_ref[pl.ds(source, rows_dev), :]
     high, low = split(queries_ref[...])
@@ -202,7 +208,7 @@
         row = best[0]
         for kind in range(1, len(best)):
             row = jnp.where(lane_chip == (chip + kind) % chunks, best[kind], row)
-        straight = crossed((pl.program_id(0) * chunks + chip) ^ origin) == (here() & 1)
+        straight = odd == parity_of(pl.program_id(0), devices) ^ parity(chip)
         out_ref[2 * chip] = jnp.where(straight, row, nothing)
         out_ref[2 * chip + 1] = jnp.where(straight, nothing, row)
 
@@ -253,7 +259,7 @@
 
 
 def gathered(blocks, stage):
-    return [exchanged(blocks, mask) for mask in stage]
+    return [exchanged(blocks, masks) for masks in stage]
 
 
 def in_hbm(*arrays):
@@ -266,7 +272,7 @@
     first, *rest = stages()
     arrived = gathered(queries, first)
     mine = (centroids, vector_ids, stored)
-    theirs = [exchanged(array, 1) for array in mine]
+    theirs = [exchanged(array, (1, 1)) for array in mine]
     places, copied = lookup(devices // 2 * rows_dev, lists, *in_hbm(list_home, probes.transpose(1, 0, 2), queries))
     blocks = jnp.concatenate([copied, *arrived], axis=0)
     for number, stage in enumerate(rest):

time: 31.4 us -> 30.7 us (0.978)
  waiting for transfers between devices: 4.76 us -> 3.32 us
  blocking collectives: 9.74 us -> 10.5 us
    ppermute x9, waiting for transfers between devices: 4.76 us -> 3.32 us  [exchanged(): lax.ppermute(value, BOTH, [(d, d ^ masks[parity(d)]) for d in range(devic...]
    all_to_all x1, blocking collectives: 9.74 us -> 10.5 us  [local(): lax.all_to_all(parts, BOTH, 0, 0, tiled=True)]
  transfers between devices with their start and end apart: 9 -> 9, of which waited for: 3 -> 2; matrix products, arithmetic and copies ran while one was open for 0% -> 0% of each run, Pallas kernels for 13% -> 14%
where the time goes in v5:
time: 30.7 us; the launch traced here: 30.5 us
  blocking collectives  10.5 us (34%)
  starting transfers between devices  9.14 us (30%)
  Pallas kernels  6.8 us (22%)
  waiting for transfers between devices  3.32 us (11%)
  between operations  0.72 us (2%)
    all_to_all x1, blocking collectives, local(): lax.all_to_all(parts, BOTH, 0, 0, tiled=True)  10.5 us
    ppermute x9, starting transfers between devices, exchanged(): lax.ppermute(value, BOTH, [(d, d ^ masks[parity(d)]) for d in range(devic...  9.14 us
    ppermute x9, waiting for transfers between devices, exchanged(): lax.ppermute(value, BOTH, [(d, d ^ masks[parity(d)]) for d in range(devic...  3.32 us
    pallas_call x2, Pallas kernels, prepare(): pl.pallas_call(copied_kernel if copied else split_lists, out_shape=(jax.S...  2.97 us
    pallas_call x1, Pallas kernels, score(): pl.pallas_call(functools.partial(score_kernel, rows_dev=rows_dev), out_sh...  1.9 us
    pallas_call x1, Pallas kernels, lookup(): pl.pallas_call(functools.partial(lookup_kernel, lists=lists, lanes=half /...  1.2 us
    pallas_call x1, Pallas kernels, finish(): pl.pallas_call(functools.partial(finish_kernel, rows_dev=rows_dev), out_s...  0.73 us
  transfers between devices with their start and end apart: 9, of which 2 were waited for; matrix products, arithmetic and copies ran while one was open for 0% of the time, Pallas kernels for 14%

profile of v5, /device:TPU:0, one launch (start us, length us, event | category | flops | bytes accessed | tf_op | source)
XLA Modules:
  0.0 30.5 jit_solution(14200426565314263949)
XLA Ops:
  0.6 0.5 %collective-permute-start.8 = (f32[4,256,768]{2,1,0:T(8,128)}, f32[4,256,768]{2,1,0:T(8,128)S(1)}, u32[]{:S(2)}, u32[]{:S(2)}) collective-permute-start(f32[4,256,768]{2,1,0:T(8,128)} %stored_hbm), channel_id=1, source_target_pairs={{0,1},{1,0},{2,3},{3,2},{4,5},{5,4},{6,7},{7,6},{8,9},{9,8},{10,11... | collective-permute-start | bytes 9437192 | tf_op jit(solution)/shard_map/ppermute | solution.py:44
  1.1 3.7 %collective-permute-start = (f32[8,768]{1,0:T(8,128)}, f32[8,768]{1,0:T(8,128)S(1)}, u32[]{:S(2)}, u32[]{:S(2)}) collective-permute-start(f32[8,768]{1,0:T(8,128)} %queries_hbm.1), channel_id=1, source_target_pairs={{0,5},{1,25},{2,26},{3,6},{4,28},{5,0},{6,3},{7,31},{8,16},{9,12},... | collective-permute-start | bytes 73736 | tf_op jit(solution)/shard_map/ppermute | solution.py:44
  4.8 1.3 %collective-permute-start.2 = (f32[8,768]{1,0:T(8,128)}, f32[8,768]{1,0:T(8,128)S(1)}, u32[]{:S(2)}, u32[]{:S(2)}) collective-permute-start(f32[8,768]{1,0:T(8,128)} %queries_hbm.1), channel_id=1, source_target_pairs={{0,6},{1,16},{2,19},{3,5},{4,21},{5,3},{6,0},{7,22},{8,25},{9,15},... | collective-permute-start | bytes 73736 | tf_op jit(solution)/shard_map/ppermute | solution.py:44
  6.2 0.0 collective-permute-start.1
  6.2 0.0 collective-permute-start.7
  6.2 1.2 %lookup.1 = (s32[3,128]{1,0:T(4,128)S(1)}, f32[8,768]{1,0:T(8,128)S(1)}) custom-call(s32[16]{0:T(128)} %home_hbm.1, s32[3,4,4]{2,1,0:T(4,128)} %bitcast.1, f32[8,768]{1,0:T(8,128)} %queries_hbm.1), custom_call_target="tpu_custom_call" | custom-call | flops 10000 | bytes 100000 | tf_op jit(solution)/shard_map/lookup/pallas_call | solution.py:103
  7.4 0.0 collective-permute-done
  7.4 0.6 %collective-permute-start.6 = (f32[32,768]{1,0:T(8,128)}, f32[32,768]{1,0:T(8,128)S(1)}, u32[]{:S(2)}, u32[]{:S(2)}) collective-permute-start(f32[32,768]{1,0:T(8,128)} %centroids_hbm), channel_id=1, source_target_pairs={{0,1},{1,0},{2,3},{3,2},{4,5},{5,4},{6,7},{7,6},{8,9},{9,8},{10,11... | collective-permute-start | bytes 294920 | tf_op jit(solution)/shard_map/ppermute | solution.py:44
  8.0 2.7 %collective-permute-done.2 = f32[8,768]{1,0:T(8,128)S(1)} collective-permute-done((f32[8,768]{1,0:T(8,128)}, f32[8,768]{1,0:T(8,128)S(1)}, u32[]{:S(2)}, u32[]{:S(2)}) %collective-permute-start.2) | collective-permute-done | bytes 24608 | tf_op jit(solution)/shard_map/ppermute | solution.py:44
  10.7 0.0 collective-permute-done.1
  10.7 0.2 collective-permute-start.5
  10.9 2.4 %collective-permute-start.4 = (f32[32,768]{1,0:T(8,128)S(1)}, f32[32,768]{1,0:T(8,128)S(1)}, u32[]{:S(2)}, u32[]{:S(2)}) collective-permute-start(f32[32,768]{1,0:T(8,128)S(1)} %pad_maximum_fusion.1), channel_id=1, source_target_pairs={{0,24},{1,2},{2,1},{3,27},{4,7},{5,29},{6,30},{7,4},{8,11},{9,17},... | collective-permute-start | bytes 294920 | tf_op jit(solution)/shard_map/ppermute | solution.py:44
  13.3 0.0 collective-permute-done.7.ids_ref
  13.3 0.4 %collective-permute-start.3 = (f32[32,768]{1,0:T(8,128)S(1)}, f32[32,768]{1,0:T(8,128)S(1)}, u32[]{:S(2)}, u32[]{:S(2)}) collective-permute-start(f32[32,768]{1,0:T(8,128)S(1)} %pad_maximum_fusion.1), channel_id=1, source_target_pairs={{0,9},{1,4},{2,7},{3,10},{4,1},{5,12},{6,15},{7,2},{8,13},{9,0},{1... | collective-permute-start | bytes 294920 | tf_op jit(solution)/shard_map/ppermute | solution.py:44
  13.7 2.1 %prepare.2 = (bf16[32,768]{1,0:T(8,128)(2,1)S(1)}, f8e4m3fn[32,768]{1,0:T(32,128)(4,1)S(1)}, s32[4,128]{1,0:T(4,128)S(1)}, bf16[4,256,768]{2,1,0:T(8,128)(2,1)S(1)}, f8e4m3fn[4,256,768]{2,1,0:T(32,128)(4,1)S(1)}) custom-call(f32[32,768]{1,0:T(8,128)} %centroids_hbm, s32[4,256]{1,0:T(4,128)} %ids_hbm, f32[4,256,768]{2,1,0:T(8,128)} %stored_hbm), custom_call_target="tpu_custom_call" | custom-call | flops 4866048 | bytes 6488064 | tf_op jit(solution)/shard_map/prepare/pallas_call | solution.py:151
  15.8 0.0 collective-permute-done.6.centroids_ref
  15.8 0.0 collective-permute-done.8.stored_ref
  15.8 0.9 %prepare.3 = (bf16[32,768]{1,0:T(8,128)(2,1)S(1)}, f8e4m3fn[32,768]{1,0:T(32,128)(4,1)S(1)}, s32[4,128]{1,0:T(4,128)S(1)}, bf16[4,256,768]{2,1,0:T(8,128)(2,1)S(1)}, f8e4m3fn[4,256,768]{2,1,0:T(32,128)(4,1)S(1)}) custom-call(f32[32,768]{1,0:T(8,128)S(1)} %collective-permute-done.6.centroids_ref, s32[4,256]{1,0:T(4,128)S(1)} %collective-permute-done.7.ids_ref, ...), custom_call_target="tpu_custom_call" | custom-call | flops 4866048 | bytes 6488064 | tf_op jit(solution)/shard_map/prepare/pallas_call | solution.py:151
  16.7 0.0 collective-permute-done.5
  16.7 0.0 collective-permute-done.4
  16.7 0.6 %collective-permute-done.3 = f32[32,768]{1,0:T(8,128)S(1)} collective-permute-done((f32[32,768]{1,0:T(8,128)S(1)}, f32[32,768]{1,0:T(8,128)S(1)}, u32[]{:S(2)}, u32[]{:S(2)}) %collective-permute-start.3) | collective-permute-done | bytes 98336 | tf_op jit(solution)/shard_map/ppermute | solution.py:44
  17.4 1.9 %score.1 = f32[32,1,128]{2,1,0:T(1,128)S(1)} custom-call(f32[128,768]{1,0:T(8,128)S(1)} %pad_maximum_fusion.blocks_ref, s32[3,128]{1,0:T(4,128)S(1)} %get-tuple-element.51.places_ref, bf16[32,768]{1,0:T(8,128)(2,1)S(1)} %get-tuple-element.52.refs_0_, f8e4m3fn[32,768]{1,0:T(32,128)(4,1)S(1)} %get-tuple-element.53.refs_1_, ...), custom_call_target="tpu_custom_call" | custom-call | flops 1660944384 | bytes 6488064 | tf_op jit(solution)/shard_map/score/pallas_call | solution.py:221
  19.3 10.5 %all_to_all.5.arrived_ref = f32[32,1,128]{2,1,0:T(1,128)S(1)} all-to-all(f32[32,1,128]{2,1,0:T(1,128)S(1)} %score.1), channel_id=1, replica_groups=mesh['group'=4,'member'=8] {'group','member'}, dimensions={0} | all-to-all | bytes 32768 | tf_op jit(solution)/shard_map/all_to_all | solution.py:287
  29.8 0.7 %finish.1 = (f32[8]{0:T(128)}, f32[3,8]{1,0:T(4,128)}) custom-call(f32[32,1,128]{2,1,0:T(1,128)S(1)} %all_to_all.5.arrived_ref), custom_call_target="tpu_custom_call" | custom-call | tf_op jit(solution)/shard_map/finish/pallas_call | solution.py:248
  (2 shorter events, 0.0 us)
Async XLA Ops:
  0.6 15.2 %collective-permute-start.8 = (f32[4,256,768]{2,1,0:T(8,128)}, f32[4,256,768]{2,1,0:T(8,128)S(1)}, u32[]{:S(2)}, u32[]{:S(2)}) collective-permute-start(f32[4,256,768]{2,1,0:T(8,128)} %stored_hbm), channel_id=1, source_target_pairs={{0,1},{1,0},{2,3},{3,2},{4,5},{5,4},{6,7},{7,6},{8,9},{9,8},{10,11... | collective-permute-start | bytes 9437192 | tf_op jit(solution)/shard_map/ppermute | solution.py:44
  1.1 6.3 %collective-permute-start = (f32[8,768]{1,0:T(8,128)}, f32[8,768]{1,0:T(8,128)S(1)}, u32[]{:S(2)}, u32[]{:S(2)}) collective-permute-start(f32[8,768]{1,0:T(8,128)} %queries_hbm.1), channel_id=1, source_target_pairs={{0,5},{1,25},{2,26},{3,6},{4,28},{5,0},{6,3},{7,31},{8,16},{9,12},... | collective-permute-start | bytes 73736 | tf_op jit(solution)/shard_map/ppermute | solution.py:44
  4.8 5.8 %collective-permute-start.2 = (f32[8,768]{1,0:T(8,128)}, f32[8,768]{1,0:T(8,128)S(1)}, u32[]{:S(2)}, u32[]{:S(2)}) collective-permute-start(f32[8,768]{1,0:T(8,128)} %queries_hbm.1), channel_id=1, source_target_pairs={{0,6},{1,16},{2,19},{3,5},{4,21},{5,3},{6,0},{7,22},{8,25},{9,15},... | collective-permute-start | bytes 73736 | tf_op jit(solution)/shard_map/ppermute | solution.py:44
  6.2 4.5 %collective-permute-start.1 = (f32[8,768]{1,0:T(8,128)}, f32[8,768]{1,0:T(8,128)S(1)}, u32[]{:S(2)}, u32[]{:S(2)}) collective-permute-start(f32[8,768]{1,0:T(8,128)} %queries_hbm.1), channel_id=1, source_target_pairs={{0,3},{1,8},{2,11},{3,0},{4,13},{5,6},{6,5},{7,14},{8,1},{9,10},{1... | collective-permute-start | bytes 73736 | tf_op jit(solution)/shard_map/ppermute | solution.py:44
  6.2 7.1 %collective-permute-start.7 = (s32[4,256]{1,0:T(4,128)}, s32[4,256]{1,0:T(4,128)S(1)}, u32[]{:S(2)}, u32[]{:S(2)}) collective-permute-start(s32[4,256]{1,0:T(4,128)} %ids_hbm), channel_id=1, source_target_pairs={{0,1},{1,0},{2,3},{3,2},{4,5},{5,4},{6,7},{7,6},{8,9},{9,8},{10,11... | collective-permute-start | bytes 12296 | tf_op jit(solution)/shard_map/ppermute | solution.py:44
  7.4 8.4 %collective-permute-start.6 = (f32[32,768]{1,0:T(8,128)}, f32[32,768]{1,0:T(8,128)S(1)}, u32[]{:S(2)}, u32[]{:S(2)}) collective-permute-start(f32[32,768]{1,0:T(8,128)} %centroids_hbm), channel_id=1, source_target_pairs={{0,1},{1,0},{2,3},{3,2},{4,5},{5,4},{6,7},{7,6},{8,9},{9,8},{10,11... | collective-permute-start | bytes 294920 | tf_op jit(solution)/shard_map/ppermute | solution.py:44
  10.7 6.0 %collective-permute-start.5 = (f32[32,768]{1,0:T(8,128)S(1)}, f32[32,768]{1,0:T(8,128)S(1)}, u32[]{:S(2)}, u32[]{:S(2)}) collective-permute-start(f32[32,768]{1,0:T(8,128)S(1)} %pad_maximum_fusion.1), channel_id=1, source_target_pairs={{0,17},{1,7},{2,4},{3,18},{4,2},{5,20},{6,23},{7,1},{8,14},{9,24},... | collective-permute-start | bytes 294920 | tf_op jit(solution)/shard_map/ppermute | solution.py:44
  10.9 5.8 %collective-permute-start.4 = (f32[32,768]{1,0:T(8,128)S(1)}, f32[32,768]{1,0:T(8,128)S(1)}, u32[]{:S(2)}, u32[]{:S(2)}) collective-permute-start(f32[32,768]{1,0:T(8,128)S(1)} %pad_maximum_fusion.1), channel_id=1, source_target_pairs={{0,24},{1,2},{2,1},{3,27},{4,7},{5,29},{6,30},{7,4},{8,11},{9,17},... | collective-permute-start | bytes 294920 | tf_op jit(solution)/shard_map/ppermute | solution.py:44
  13.3 4.0 %collective-permute-start.3 = (f32[32,768]{1,0:T(8,128)S(1)}, f32[32,768]{1,0:T(8,128)S(1)}, u32[]{:S(2)}, u32[]{:S(2)}) collective-permute-start(f32[32,768]{1,0:T(8,128)S(1)} %pad_maximum_fusion.1), channel_id=1, source_target_pairs={{0,9},{1,4},{2,7},{3,10},{4,1},{5,12},{6,15},{7,2},{8,13},{9,0},{1... | collective-permute-start | bytes 294920 | tf_op jit(solution)/shard_map/ppermute | solution.py:44

commit v6 on v5

--- a/solution.py
+++ b/solution.py
@@ -194,9 +194,15 @@
         centers_ref, centers_low_ref, counts_ref, vectors_ref, vectors_low_ref = halves[5 * side : 5 * side + 5]
         lists, length = vectors_ref.shape[:2]
         place = lax.broadcasted_iota(jnp.int32, (length, TILE), 0)
-        best[0] = jnp.maximum(best[0], jnp.max(scores(centers_ref, centers_low_ref), axis=0, keepdims=True))
         for slot in range(lists):
-            usable = jnp.where(place < counts_ref[pl.ds(slot, 1), :], scores(vectors_ref.at[slot], vectors_low_ref.at[slot]), LOWEST)
+            high, low = vectors_ref[slot], vectors_low_ref[slot]
+            if side == 1 and slot == lists - 1:
+                high = jnp.concatenate([high, halves[0][...], centers_ref[...]], axis=0)
+                low = jnp.concatenate([low, halves[1][...], centers_low_ref[...]], axis=0)
+            found = scores(high, low)
+            if side == 1 and slot == lists - 1:
+                best[0] = jnp.max(found[length:], axis=0, keepdims=True)
+            usable = jnp.where(place < counts_ref[pl.ds(slot, 1), :], found[:length], LOWEST)
             found = jnp.max(usable, axis=0, keepdims=True)
             for step in range(places_ref.shape[0]):
                 chosen = jnp.where(places_ref[pl.ds(step, 1), :] == slot, found, LOWEST)

time: 30.7 us -> 30.5 us (level)
  no operation moved by 1% of the time
where the time goes in v6:
time: 30.5 us; the launch traced here: 30.3 us
  blocking collectives  10.5 us (34%)
  starting transfers between devices  9.14 us (30%)
  Pallas kernels  6.62 us (22%)
  waiting for transfers between devices  3.32 us (11%)
  between operations  0.72 us (2%)
    all_to_all x1, blocking collectives, local(): lax.all_to_all(parts, BOTH, 0, 0, tiled=True)  10.5 us
    ppermute x9, starting transfers between devices, exchanged(): lax.ppermute(value, BOTH, [(d, d ^ masks[parity(d)]) for d in range(devic...  9.14 us
    ppermute x9, waiting for transfers between devices, exchanged(): lax.ppermute(value, BOTH, [(d, d ^ masks[parity(d)]) for d in range(devic...  3.32 us
    pallas_call x2, Pallas kernels, prepare(): pl.pallas_call(copied_kernel if copied else split_lists, out_shape=(jax.S...  2.97 us
    pallas_call x1, Pallas kernels, score(): pl.pallas_call(functools.partial(score_kernel, rows_dev=rows_dev), out_sh...  1.72 us
    pallas_call x1, Pallas kernels, lookup(): pl.pallas_call(functools.partial(lookup_kernel, lists=lists, lanes=half /...  1.2 us
    pallas_call x1, Pallas kernels, finish(): pl.pallas_call(functools.partial(finish_kernel, rows_dev=rows_dev), out_s...  0.73 us
  transfers between devices with their start and end apart: 9, of which 2 were waited for; matrix products, arithmetic and copies ran while one was open for 0% of the time, Pallas kernels for 14%

profile of v6, /device:TPU:0, one launch (start us, length us, event | category | flops | bytes accessed | tf_op | source)
XLA Modules:
  0.0 30.3 jit_solution(5989583377117020491)
XLA Ops:
  0.6 0.5 %collective-permute-start.8 = (f32[4,256,768]{2,1,0:T(8,128)}, f32[4,256,768]{2,1,0:T(8,128)S(1)}, u32[]{:S(2)}, u32[]{:S(2)}) collective-permute-start(f32[4,256,768]{2,1,0:T(8,128)} %stored_hbm), channel_id=1, source_target_pairs={{0,1},{1,0},{2,3},{3,2},{4,5},{5,4},{6,7},{7,6},{8,9},{9,8},{10,11... | collective-permute-start | bytes 9437192 | tf_op jit(solution)/shard_map/ppermute | solution.py:44
  1.1 3.7 %collective-permute-start = (f32[8,768]{1,0:T(8,128)}, f32[8,768]{1,0:T(8,128)S(1)}, u32[]{:S(2)}, u32[]{:S(2)}) collective-permute-start(f32[8,768]{1,0:T(8,128)} %queries_hbm.1), channel_id=1, source_target_pairs={{0,5},{1,25},{2,26},{3,6},{4,28},{5,0},{6,3},{7,31},{8,16},{9,12},... | collective-permute-start | bytes 73736 | tf_op jit(solution)/shard_map/ppermute | solution.py:44
  4.8 1.3 %collective-permute-start.2 = (f32[8,768]{1,0:T(8,128)}, f32[8,768]{1,0:T(8,128)S(1)}, u32[]{:S(2)}, u32[]{:S(2)}) collective-permute-start(f32[8,768]{1,0:T(8,128)} %queries_hbm.1), channel_id=1, source_target_pairs={{0,6},{1,16},{2,19},{3,5},{4,21},{5,3},{6,0},{7,22},{8,25},{9,15},... | collective-permute-start | bytes 73736 | tf_op jit(solution)/shard_map/ppermute | solution.py:44
  6.2 0.0 collective-permute-start.1
  6.2 0.0 collective-permute-start.7
  6.2 1.2 %lookup.1 = (s32[3,128]{1,0:T(4,128)S(1)}, f32[8,768]{1,0:T(8,128)S(1)}) custom-call(s32[16]{0:T(128)} %home_hbm.1, s32[3,4,4]{2,1,0:T(4,128)} %bitcast.1, f32[8,768]{1,0:T(8,128)} %queries_hbm.1), custom_call_target="tpu_custom_call" | custom-call | flops 10000 | bytes 100000 | tf_op jit(solution)/shard_map/lookup/pallas_call | solution.py:103
  7.4 0.0 collective-permute-done
  7.4 0.6 %collective-permute-start.6 = (f32[32,768]{1,0:T(8,128)}, f32[32,768]{1,0:T(8,128)S(1)}, u32[]{:S(2)}, u32[]{:S(2)}) collective-permute-start(f32[32,768]{1,0:T(8,128)} %centroids_hbm), channel_id=1, source_target_pairs={{0,1},{1,0},{2,3},{3,2},{4,5},{5,4},{6,7},{7,6},{8,9},{9,8},{10,11... | collective-permute-start | bytes 294920 | tf_op jit(solution)/shard_map/ppermute | solution.py:44
  8.0 2.7 %collective-permute-done.2 = f32[8,768]{1,0:T(8,128)S(1)} collective-permute-done((f32[8,768]{1,0:T(8,128)}, f32[8,768]{1,0:T(8,128)S(1)}, u32[]{:S(2)}, u32[]{:S(2)}) %collective-permute-start.2) | collective-permute-done | bytes 24608 | tf_op jit(solution)/shard_map/ppermute | solution.py:44
  10.7 0.0 collective-permute-done.1
  10.7 0.2 collective-permute-start.5
  10.9 2.4 %collective-permute-start.4 = (f32[32,768]{1,0:T(8,128)S(1)}, f32[32,768]{1,0:T(8,128)S(1)}, u32[]{:S(2)}, u32[]{:S(2)}) collective-permute-start(f32[32,768]{1,0:T(8,128)S(1)} %pad_maximum_fusion.1), channel_id=1, source_target_pairs={{0,24},{1,2},{2,1},{3,27},{4,7},{5,29},{6,30},{7,4},{8,11},{9,17},... | collective-permute-start | bytes 294920 | tf_op jit(solution)/shard_map/ppermute | solution.py:44
  13.3 0.0 collective-permute-done.7.ids_ref
  13.3 0.4 %collective-permute-start.3 = (f32[32,768]{1,0:T(8,128)S(1)}, f32[32,768]{1,0:T(8,128)S(1)}, u32[]{:S(2)}, u32[]{:S(2)}) collective-permute-start(f32[32,768]{1,0:T(8,128)S(1)} %pad_maximum_fusion.1), channel_id=1, source_target_pairs={{0,9},{1,4},{2,7},{3,10},{4,1},{5,12},{6,15},{7,2},{8,13},{9,0},{1... | collective-permute-start | bytes 294920 | tf_op jit(solution)/shard_map/ppermute | solution.py:44
  13.7 2.1 %prepare.2 = (bf16[32,768]{1,0:T(8,128)(2,1)S(1)}, f8e4m3fn[32,768]{1,0:T(32,128)(4,1)S(1)}, s32[4,128]{1,0:T(4,128)S(1)}, bf16[4,256,768]{2,1,0:T(8,128)(2,1)S(1)}, f8e4m3fn[4,256,768]{2,1,0:T(32,128)(4,1)S(1)}) custom-call(f32[32,768]{1,0:T(8,128)} %centroids_hbm, s32[4,256]{1,0:T(4,128)} %ids_hbm, f32[4,256,768]{2,1,0:T(8,128)} %stored_hbm), custom_call_target="tpu_custom_call" | custom-call | flops 4866048 | bytes 6488064 | tf_op jit(solution)/shard_map/prepare/pallas_call | solution.py:151
  15.8 0.0 collective-permute-done.6.centroids_ref
  15.8 0.0 collective-permute-done.8.stored_ref
  15.8 0.9 %prepare.3 = (bf16[32,768]{1,0:T(8,128)(2,1)S(1)}, f8e4m3fn[32,768]{1,0:T(32,128)(4,1)S(1)}, s32[4,128]{1,0:T(4,128)S(1)}, bf16[4,256,768]{2,1,0:T(8,128)(2,1)S(1)}, f8e4m3fn[4,256,768]{2,1,0:T(32,128)(4,1)S(1)}) custom-call(f32[32,768]{1,0:T(8,128)S(1)} %collective-permute-done.6.centroids_ref, s32[4,256]{1,0:T(4,128)S(1)} %collective-permute-done.7.ids_ref, ...), custom_call_target="tpu_custom_call" | custom-call | flops 4866048 | bytes 6488064 | tf_op jit(solution)/shard_map/prepare/pallas_call | solution.py:151
  16.7 0.0 collective-permute-done.5
  16.7 0.0 collective-permute-done.4
  16.7 0.6 %collective-permute-done.3 = f32[32,768]{1,0:T(8,128)S(1)} collective-permute-done((f32[32,768]{1,0:T(8,128)S(1)}, f32[32,768]{1,0:T(8,128)S(1)}, u32[]{:S(2)}, u32[]{:S(2)}) %collective-permute-start.3) | collective-permute-done | bytes 98336 | tf_op jit(solution)/shard_map/ppermute | solution.py:44
  17.4 1.7 %score.1 = f32[32,1,128]{2,1,0:T(1,128)S(1)} custom-call(f32[128,768]{1,0:T(8,128)S(1)} %pad_maximum_fusion.blocks_ref, s32[3,128]{1,0:T(4,128)S(1)} %get-tuple-element.51.places_ref, bf16[32,768]{1,0:T(8,128)(2,1)S(1)} %get-tuple-element.52.refs_0_, f8e4m3fn[32,768]{1,0:T(32,128)(4,1)S(1)} %get-tuple-element.53.refs_1_, ...), custom_call_target="tpu_custom_call" | custom-call | flops 1660944384 | bytes 6488064 | tf_op jit(solution)/shard_map/score/pallas_call | solution.py:227
  19.1 10.5 %all_to_all.5.arrived_ref = f32[32,1,128]{2,1,0:T(1,128)S(1)} all-to-all(f32[32,1,128]{2,1,0:T(1,128)S(1)} %score.1), channel_id=1, replica_groups=mesh['group'=4,'member'=8] {'group','member'}, dimensions={0} | all-to-all | bytes 32768 | tf_op jit(solution)/shard_map/all_to_all | solution.py:293
  29.6 0.7 %finish.1 = (f32[8]{0:T(128)}, f32[3,8]{1,0:T(4,128)}) custom-call(f32[32,1,128]{2,1,0:T(1,128)S(1)} %all_to_all.5.arrived_ref), custom_call_target="tpu_custom_call" | custom-call | tf_op jit(solution)/shard_map/finish/pallas_call | solution.py:254
  (2 shorter events, 0.0 us)
Async XLA Ops:
  0.6 15.2 %collective-permute-start.8 = (f32[4,256,768]{2,1,0:T(8,128)}, f32[4,256,768]{2,1,0:T(8,128)S(1)}, u32[]{:S(2)}, u32[]{:S(2)}) collective-permute-start(f32[4,256,768]{2,1,0:T(8,128)} %stored_hbm), channel_id=1, source_target_pairs={{0,1},{1,0},{2,3},{3,2},{4,5},{5,4},{6,7},{7,6},{8,9},{9,8},{10,11... | collective-permute-start | bytes 9437192 | tf_op jit(solution)/shard_map/ppermute | solution.py:44
  1.1 6.3 %collective-permute-start = (f32[8,768]{1,0:T(8,128)}, f32[8,768]{1,0:T(8,128)S(1)}, u32[]{:S(2)}, u32[]{:S(2)}) collective-permute-start(f32[8,768]{1,0:T(8,128)} %queries_hbm.1), channel_id=1, source_target_pairs={{0,5},{1,25},{2,26},{3,6},{4,28},{5,0},{6,3},{7,31},{8,16},{9,12},... | collective-permute-start | bytes 73736 | tf_op jit(solution)/shard_map/ppermute | solution.py:44
  4.8 5.8 %collective-permute-start.2 = (f32[8,768]{1,0:T(8,128)}, f32[8,768]{1,0:T(8,128)S(1)}, u32[]{:S(2)}, u32[]{:S(2)}) collective-permute-start(f32[8,768]{1,0:T(8,128)} %queries_hbm.1), channel_id=1, source_target_pairs={{0,6},{1,16},{2,19},{3,5},{4,21},{5,3},{6,0},{7,22},{8,25},{9,15},... | collective-permute-start | bytes 73736 | tf_op jit(solution)/shard_map/ppermute | solution.py:44
  6.2 4.5 %collective-permute-start.1 = (f32[8,768]{1,0:T(8,128)}, f32[8,768]{1,0:T(8,128)S(1)}, u32[]{:S(2)}, u32[]{:S(2)}) collective-permute-start(f32[8,768]{1,0:T(8,128)} %queries_hbm.1), channel_id=1, source_target_pairs={{0,3},{1,8},{2,11},{3,0},{4,13},{5,6},{6,5},{7,14},{8,1},{9,10},{1... | collective-permute-start | bytes 73736 | tf_op jit(solution)/shard_map/ppermute | solution.py:44
  6.2 7.1 %collective-permute-start.7 = (s32[4,256]{1,0:T(4,128)}, s32[4,256]{1,0:T(4,128)S(1)}, u32[]{:S(2)}, u32[]{:S(2)}) collective-permute-start(s32[4,256]{1,0:T(4,128)} %ids_hbm), channel_id=1, source_target_pairs={{0,1},{1,0},{2,3},{3,2},{4,5},{5,4},{6,7},{7,6},{8,9},{9,8},{10,11... | collective-permute-start | bytes 12296 | tf_op jit(solution)/shard_map/ppermute | solution.py:44
  7.4 8.4 %collective-permute-start.6 = (f32[32,768]{1,0:T(8,128)}, f32[32,768]{1,0:T(8,128)S(1)}, u32[]{:S(2)}, u32[]{:S(2)}) collective-permute-start(f32[32,768]{1,0:T(8,128)} %centroids_hbm), channel_id=1, source_target_pairs={{0,1},{1,0},{2,3},{3,2},{4,5},{5,4},{6,7},{7,6},{8,9},{9,8},{10,11... | collective-permute-start | bytes 294920 | tf_op jit(solution)/shard_map/ppermute | solution.py:44
  10.7 6.0 %collective-permute-start.5 = (f32[32,768]{1,0:T(8,128)S(1)}, f32[32,768]{1,0:T(8,128)S(1)}, u32[]{:S(2)}, u32[]{:S(2)}) collective-permute-start(f32[32,768]{1,0:T(8,128)S(1)} %pad_maximum_fusion.1), channel_id=1, source_target_pairs={{0,17},{1,7},{2,4},{3,18},{4,2},{5,20},{6,23},{7,1},{8,14},{9,24},... | collective-permute-start | bytes 294920 | tf_op jit(solution)/shard_map/ppermute | solution.py:44
  10.9 5.8 %collective-permute-start.4 = (f32[32,768]{1,0:T(8,128)S(1)}, f32[32,768]{1,0:T(8,128)S(1)}, u32[]{:S(2)}, u32[]{:S(2)}) collective-permute-start(f32[32,768]{1,0:T(8,128)S(1)} %pad_maximum_fusion.1), channel_id=1, source_target_pairs={{0,24},{1,2},{2,1},{3,27},{4,7},{5,29},{6,30},{7,4},{8,11},{9,17},... | collective-permute-start | bytes 294920 | tf_op jit(solution)/shard_map/ppermute | solution.py:44
  13.3 4.0 %collective-permute-start.3 = (f32[32,768]{1,0:T(8,128)S(1)}, f32[32,768]{1,0:T(8,128)S(1)}, u32[]{:S(2)}, u32[]{:S(2)}) collective-permute-start(f32[32,768]{1,0:T(8,128)S(1)} %pad_maximum_fusion.1), channel_id=1, source_target_pairs={{0,9},{1,4},{2,7},{3,10},{4,1},{5,12},{6,15},{7,2},{8,13},{9,0},{1... | collective-permute-start | bytes 294920 | tf_op jit(solution)/shard_map/ppermute | solution.py:44

commit v7 on v6

--- a/solution.py
+++ b/solution.py
@@ -167,7 +167,7 @@
 
 
 def score_kernel(blocks_ref, places_ref, *refs, rows_dev):
-    *halves, out_ref, queries_ref, parts_ref, eighth_ref = refs
+    *halves, out_ref, parts_ref, eighth_ref = refs
     devices = lax.axis_size("group") * lax.axis_size("member")
     odd = parity_of(here(), devices)
     chunks = TILE // rows_dev
@@ -176,13 +176,19 @@
         return jnp.where(odd == 1, position(chip, 1), position(chip, 0))
 
     first = place_of(here() >> 1)
-    for chunk in range(chunks):
-        offset = place_of(chunk if blocks_ref.shape[0] == TILE else pl.program_id(0) * chunks + chunk)
-        source = pl.multiple_of((first ^ offset) * rows_dev, rows_dev)
-        queries_ref[pl.ds(chunk * rows_dev, rows_dev), :] = blocks_ref[pl.ds(source, rows_dev), :]
-    high, low = split(queries_ref[...])
-    parts_ref[:TILE], parts_ref[TILE:] = high, low.astype(jnp.bfloat16)
-    eighth_ref[...] = queries_ref[...].astype(EIGHT)
+    several = 32 // rows_dev
+    for group in range(chunks // several):
+        blocks = []
+        for chunk in range(group * several, (group + 1) * several):
+            offset = place_of(chunk if blocks_ref.shape[0] == TILE else pl.program_id(0) * chunks + chunk)
+            source = pl.multiple_of((first ^ offset) * rows_dev, rows_dev)
+            blocks.append(blocks_ref[pl.ds(source, rows_dev), :])
+        queries = jnp.concatenate(blocks, axis=0)
+        at = group * several * rows_dev
+        high, low = split(queries)
+        parts_ref[pl.ds(at, 32), :] = high
+        parts_ref[pl.ds(TILE + at, 32), :] = low.astype(jnp.bfloat16)
+        eighth_ref[pl.ds(at, 32), :] = queries.astype(EIGHT)
 
     def scores(vectors, vectors_low):
         terms = lax.dot_general(vectors[...], parts_ref[...], NT, preferred_element_type=jnp.float32)
@@ -231,7 +237,6 @@
         in_specs=[WHOLE, pl.BlockSpec((kinds - 1, TILE), lambda i: (0, i)), *[WHOLE] * len(halves)],
         out_specs=pl.BlockSpec((devices, 1, TILE), lambda i: (i, 0, 0)),
         scratch_shapes=[
-            pltpu.VMEM((TILE, depth), jnp.float32),
             pltpu.VMEM((2 * TILE, depth), jnp.bfloat16),
             pltpu.VMEM((TILE, depth), EIGHT),
         ],

time: 30.5 us -> 30.5 us (level)
  no operation moved by 1% of the time
where the time goes in v7:
time: 30.5 us; the launch traced here: 30.3 us
  blocking collectives  10.5 us (34%)
  starting transfers between devices  9.14 us (30%)
  Pallas kernels  6.62 us (22%)
  waiting for transfers between devices  3.32 us (11%)
  between operations  0.72 us (2%)
    all_to_all x1, blocking collectives, local(): lax.all_to_all(parts, BOTH, 0, 0, tiled=True)  10.5 us
    ppermute x9, starting transfers between devices, exchanged(): lax.ppermute(value, BOTH, [(d, d ^ masks[parity(d)]) for d in range(devic...  9.14 us
    ppermute x9, waiting for transfers between devices, exchanged(): lax.ppermute(value, BOTH, [(d, d ^ masks[parity(d)]) for d in range(devic...  3.32 us
    pallas_call x2, Pallas kernels, prepare(): pl.pallas_call(copied_kernel if copied else split_lists, out_shape=(jax.S...  2.97 us
    pallas_call x1, Pallas kernels, score(): pl.pallas_call(functools.partial(score_kernel, rows_dev=rows_dev), out_sh...  1.72 us
    pallas_call x1, Pallas kernels, lookup(): pl.pallas_call(functools.partial(lookup_kernel, lists=lists, lanes=half /...  1.2 us
    pallas_call x1, Pallas kernels, finish(): pl.pallas_call(functools.partial(finish_kernel, rows_dev=rows_dev), out_s...  0.73 us
  transfers between devices with their start and end apart: 9, of which 2 were waited for; matrix products, arithmetic and copies ran while one was open for 0% of the time, Pallas kernels for 14%

profile of v7, /device:TPU:0, one launch (start us, length us, event | category | flops | bytes accessed | tf_op | source)
XLA Modules:
  0.0 30.3 jit_solution(5989583377117020491)
XLA Ops:
  0.6 0.5 %collective-permute-start.8 = (f32[4,256,768]{2,1,0:T(8,128)}, f32[4,256,768]{2,1,0:T(8,128)S(1)}, u32[]{:S(2)}, u32[]{:S(2)}) collective-permute-start(f32[4,256,768]{2,1,0:T(8,128)} %stored_hbm), channel_id=1, source_target_pairs={{0,1},{1,0},{2,3},{3,2},{4,5},{5,4},{6,7},{7,6},{8,9},{9,8},{10,11... | collective-permute-start | bytes 9437192 | tf_op jit(solution)/shard_map/ppermute | solution.py:44
  1.1 3.7 %collective-permute-start = (f32[8,768]{1,0:T(8,128)}, f32[8,768]{1,0:T(8,128)S(1)}, u32[]{:S(2)}, u32[]{:S(2)}) collective-permute-start(f32[8,768]{1,0:T(8,128)} %queries_hbm.1), channel_id=1, source_target_pairs={{0,5},{1,25},{2,26},{3,6},{4,28},{5,0},{6,3},{7,31},{8,16},{9,12},... | collective-permute-start | bytes 73736 | tf_op jit(solution)/shard_map/ppermute | solution.py:44
  4.8 1.3 %collective-permute-start.2 = (f32[8,768]{1,0:T(8,128)}, f32[8,768]{1,0:T(8,128)S(1)}, u32[]{:S(2)}, u32[]{:S(2)}) collective-permute-start(f32[8,768]{1,0:T(8,128)} %queries_hbm.1), channel_id=1, source_target_pairs={{0,6},{1,16},{2,19},{3,5},{4,21},{5,3},{6,0},{7,22},{8,25},{9,15},... | collective-permute-start | bytes 73736 | tf_op jit(solution)/shard_map/ppermute | solution.py:44
  6.2 0.0 collective-permute-start.1
  6.2 0.0 collective-permute-start.7
  6.2 1.2 %lookup.1 = (s32[3,128]{1,0:T(4,128)S(1)}, f32[8,768]{1,0:T(8,128)S(1)}) custom-call(s32[16]{0:T(128)} %home_hbm.1, s32[3,4,4]{2,1,0:T(4,128)} %bitcast.1, f32[8,768]{1,0:T(8,128)} %queries_hbm.1), custom_call_target="tpu_custom_call" | custom-call | flops 10000 | bytes 100000 | tf_op jit(solution)/shard_map/lookup/pallas_call | solution.py:103
  7.4 0.0 collective-permute-done
  7.4 0.6 %collective-permute-start.6 = (f32[32,768]{1,0:T(8,128)}, f32[32,768]{1,0:T(8,128)S(1)}, u32[]{:S(2)}, u32[]{:S(2)}) collective-permute-start(f32[32,768]{1,0:T(8,128)} %centroids_hbm), channel_id=1, source_target_pairs={{0,1},{1,0},{2,3},{3,2},{4,5},{5,4},{6,7},{7,6},{8,9},{9,8},{10,11... | collective-permute-start | bytes 294920 | tf_op jit(solution)/shard_map/ppermute | solution.py:44
  8.0 2.7 %collective-permute-done.2 = f32[8,768]{1,0:T(8,128)S(1)} collective-permute-done((f32[8,768]{1,0:T(8,128)}, f32[8,768]{1,0:T(8,128)S(1)}, u32[]{:S(2)}, u32[]{:S(2)}) %collective-permute-start.2) | collective-permute-done | bytes 24608 | tf_op jit(solution)/shard_map/ppermute | solution.py:44
  10.7 0.0 collective-permute-done.1
  10.7 0.2 collective-permute-start.5
  10.9 2.4 %collective-permute-start.4 = (f32[32,768]{1,0:T(8,128)S(1)}, f32[32,768]{1,0:T(8,128)S(1)}, u32[]{:S(2)}, u32[]{:S(2)}) collective-permute-start(f32[32,768]{1,0:T(8,128)S(1)} %pad_maximum_fusion.1), channel_id=1, source_target_pairs={{0,24},{1,2},{2,1},{3,27},{4,7},{5,29},{6,30},{7,4},{8,11},{9,17},... | collective-permute-start | bytes 294920 | tf_op jit(solution)/shard_map/ppermute | solution.py:44
  13.3 0.0 collective-permute-done.7.ids_ref
  13.3 0.4 %collective-permute-start.3 = (f32[32,768]{1,0:T(8,128)S(1)}, f32[32,768]{1,0:T(8,128)S(1)}, u32[]{:S(2)}, u32[]{:S(2)}) collective-permute-start(f32[32,768]{1,0:T(8,128)S(1)} %pad_maximum_fusion.1), channel_id=1, source_target_pairs={{0,9},{1,4},{2,7},{3,10},{4,1},{5,12},{6,15},{7,2},{8,13},{9,0},{1... | collective-permute-start | bytes 294920 | tf_op jit(solution)/shard_map/ppermute | solution.py:44
  13.7 2.1 %prepare.2 = (bf16[32,768]{1,0:T(8,128)(2,1)S(1)}, f8e4m3fn[32,768]{1,0:T(32,128)(4,1)S(1)}, s32[4,128]{1,0:T(4,128)S(1)}, bf16[4,256,768]{2,1,0:T(8,128)(2,1)S(1)}, f8e4m3fn[4,256,768]{2,1,0:T(32,128)(4,1)S(1)}) custom-call(f32[32,768]{1,0:T(8,128)} %centroids_hbm, s32[4,256]{1,0:T(4,128)} %ids_hbm, f32[4,256,768]{2,1,0:T(8,128)} %stored_hbm), custom_call_target="tpu_custom_call" | custom-call | flops 4866048 | bytes 6488064 | tf_op jit(solution)/shard_map/prepare/pallas_call | solution.py:151
  15.8 0.0 collective-permute-done.6.centroids_ref
  15.8 0.0 collective-permute-done.8.stored_ref
  15.8 0.9 %prepare.3 = (bf16[32,768]{1,0:T(8,128)(2,1)S(1)}, f8e4m3fn[32,768]{1,0:T(32,128)(4,1)S(1)}, s32[4,128]{1,0:T(4,128)S(1)}, bf16[4,256,768]{2,1,0:T(8,128)(2,1)S(1)}, f8e4m3fn[4,256,768]{2,1,0:T(32,128)(4,1)S(1)}) custom-call(f32[32,768]{1,0:T(8,128)S(1)} %collective-permute-done.6.centroids_ref, s32[4,256]{1,0:T(4,128)S(1)} %collective-permute-done.7.ids_ref, ...), custom_call_target="tpu_custom_call" | custom-call | flops 4866048 | bytes 6488064 | tf_op jit(solution)/shard_map/prepare/pallas_call | solution.py:151
  16.7 0.0 collective-permute-done.5
  16.7 0.0 collective-permute-done.4
  16.7 0.6 %collective-permute-done.3 = f32[32,768]{1,0:T(8,128)S(1)} collective-permute-done((f32[32,768]{1,0:T(8,128)S(1)}, f32[32,768]{1,0:T(8,128)S(1)}, u32[]{:S(2)}, u32[]{:S(2)}) %collective-permute-start.3) | collective-permute-done | bytes 98336 | tf_op jit(solution)/shard_map/ppermute | solution.py:44
  17.4 1.7 %score.1 = f32[32,1,128]{2,1,0:T(1,128)S(1)} custom-call(f32[128,768]{1,0:T(8,128)S(1)} %pad_maximum_fusion.blocks_ref, s32[3,128]{1,0:T(4,128)S(1)} %get-tuple-element.51.places_ref, bf16[32,768]{1,0:T(8,128)(2,1)S(1)} %get-tuple-element.52.refs_0_, f8e4m3fn[32,768]{1,0:T(32,128)(4,1)S(1)} %get-tuple-element.53.refs_1_, ...), custom_call_target="tpu_custom_call" | custom-call | flops 1660944384 | bytes 6488064 | tf_op jit(solution)/shard_map/score/pallas_call | solution.py:233
  19.1 10.5 %all_to_all.5.arrived_ref = f32[32,1,128]{2,1,0:T(1,128)S(1)} all-to-all(f32[32,1,128]{2,1,0:T(1,128)S(1)} %score.1), channel_id=1, replica_groups=mesh['group'=4,'member'=8] {'group','member'}, dimensions={0} | all-to-all | bytes 32768 | tf_op jit(solution)/shard_map/all_to_all | solution.py:298
  29.6 0.7 %finish.1 = (f32[8]{0:T(128)}, f32[3,8]{1,0:T(4,128)}) custom-call(f32[32,1,128]{2,1,0:T(1,128)S(1)} %all_to_all.5.arrived_ref), custom_call_target="tpu_custom_call" | custom-call | tf_op jit(solution)/shard_map/finish/pallas_call | solution.py:259
  (2 shorter events, 0.0 us)
Async XLA Ops:
  0.6 15.2 %collective-permute-start.8 = (f32[4,256,768]{2,1,0:T(8,128)}, f32[4,256,768]{2,1,0:T(8,128)S(1)}, u32[]{:S(2)}, u32[]{:S(2)}) collective-permute-start(f32[4,256,768]{2,1,0:T(8,128)} %stored_hbm), channel_id=1, source_target_pairs={{0,1},{1,0},{2,3},{3,2},{4,5},{5,4},{6,7},{7,6},{8,9},{9,8},{10,11... | collective-permute-start | bytes 9437192 | tf_op jit(solution)/shard_map/ppermute | solution.py:44
  1.1 6.3 %collective-permute-start = (f32[8,768]{1,0:T(8,128)}, f32[8,768]{1,0:T(8,128)S(1)}, u32[]{:S(2)}, u32[]{:S(2)}) collective-permute-start(f32[8,768]{1,0:T(8,128)} %queries_hbm.1), channel_id=1, source_target_pairs={{0,5},{1,25},{2,26},{3,6},{4,28},{5,0},{6,3},{7,31},{8,16},{9,12},... | collective-permute-start | bytes 73736 | tf_op jit(solution)/shard_map/ppermute | solution.py:44
  4.8 5.8 %collective-permute-start.2 = (f32[8,768]{1,0:T(8,128)}, f32[8,768]{1,0:T(8,128)S(1)}, u32[]{:S(2)}, u32[]{:S(2)}) collective-permute-start(f32[8,768]{1,0:T(8,128)} %queries_hbm.1), channel_id=1, source_target_pairs={{0,6},{1,16},{2,19},{3,5},{4,21},{5,3},{6,0},{7,22},{8,25},{9,15},... | collective-permute-start | bytes 73736 | tf_op jit(solution)/shard_map/ppermute | solution.py:44
  6.2 4.5 %collective-permute-start.1 = (f32[8,768]{1,0:T(8,128)}, f32[8,768]{1,0:T(8,128)S(1)}, u32[]{:S(2)}, u32[]{:S(2)}) collective-permute-start(f32[8,768]{1,0:T(8,128)} %queries_hbm.1), channel_id=1, source_target_pairs={{0,3},{1,8},{2,11},{3,0},{4,13},{5,6},{6,5},{7,14},{8,1},{9,10},{1... | collective-permute-start | bytes 73736 | tf_op jit(solution)/shard_map/ppermute | solution.py:44
  6.2 7.1 %collective-permute-start.7 = (s32[4,256]{1,0:T(4,128)}, s32[4,256]{1,0:T(4,128)S(1)}, u32[]{:S(2)}, u32[]{:S(2)}) collective-permute-start(s32[4,256]{1,0:T(4,128)} %ids_hbm), channel_id=1, source_target_pairs={{0,1},{1,0},{2,3},{3,2},{4,5},{5,4},{6,7},{7,6},{8,9},{9,8},{10,11... | collective-permute-start | bytes 12296 | tf_op jit(solution)/shard_map/ppermute | solution.py:44
  7.4 8.4 %collective-permute-start.6 = (f32[32,768]{1,0:T(8,128)}, f32[32,768]{1,0:T(8,128)S(1)}, u32[]{:S(2)}, u32[]{:S(2)}) collective-permute-start(f32[32,768]{1,0:T(8,128)} %centroids_hbm), channel_id=1, source_target_pairs={{0,1},{1,0},{2,3},{3,2},{4,5},{5,4},{6,7},{7,6},{8,9},{9,8},{10,11... | collective-permute-start | bytes 294920 | tf_op jit(solution)/shard_map/ppermute | solution.py:44
  10.7 6.0 %collective-permute-start.5 = (f32[32,768]{1,0:T(8,128)S(1)}, f32[32,768]{1,0:T(8,128)S(1)}, u32[]{:S(2)}, u32[]{:S(2)}) collective-permute-start(f32[32,768]{1,0:T(8,128)S(1)} %pad_maximum_fusion.1), channel_id=1, source_target_pairs={{0,17},{1,7},{2,4},{3,18},{4,2},{5,20},{6,23},{7,1},{8,14},{9,24},... | collective-permute-start | bytes 294920 | tf_op jit(solution)/shard_map/ppermute | solution.py:44
  10.9 5.8 %collective-permute-start.4 = (f32[32,768]{1,0:T(8,128)S(1)}, f32[32,768]{1,0:T(8,128)S(1)}, u32[]{:S(2)}, u32[]{:S(2)}) collective-permute-start(f32[32,768]{1,0:T(8,128)S(1)} %pad_maximum_fusion.1), channel_id=1, source_target_pairs={{0,24},{1,2},{2,1},{3,27},{4,7},{5,29},{6,30},{7,4},{8,11},{9,17},... | collective-permute-start | bytes 294920 | tf_op jit(solution)/shard_map/ppermute | solution.py:44
  13.3 4.0 %collective-permute-start.3 = (f32[32,768]{1,0:T(8,128)S(1)}, f32[32,768]{1,0:T(8,128)S(1)}, u32[]{:S(2)}, u32[]{:S(2)}) collective-permute-start(f32[32,768]{1,0:T(8,128)S(1)} %pad_maximum_fusion.1), channel_id=1, source_target_pairs={{0,9},{1,4},{2,7},{3,10},{4,1},{5,12},{6,15},{7,2},{8,13},{9,0},{1... | collective-permute-start | bytes 294920 | tf_op jit(solution)/shard_map/ppermute | solution.py:44
